TPU v7x, 32 devices: a whole 2x2x4 slice. The times are simulated.
32 devices in a mesh: px: 4 (over y, core), py: 8 (over z, x).
Axes of the slice: x: 2, y: 2, z: 4, core: 2. Of those that a mesh axis runs over, the one named last changes fastest.
Arguments:
- kappa: bfloat16 [76800, 128], P(('px', 'py')), may hold values from -6 to 6
- send_list: int32 [32, 32, 384], P(('px', 'py')), may hold values from 0 to 2399, as said below
- dest_slot: int32 [32, 32, 384], P(('px', 'py')), may hold values from 0 to 2047, as said below
- send_count: int32 [32, 32], P(('px', 'py')), may hold values from 0 to 384, as said below
Outputs:
- flexion: float32 [4, 2048, 4096], P(None, 'px', 'py')
Inputs may be any that keep to these rules, and one draw needn't show every extreme that they name: For k < send_count[a, d], send_list[a, d, k] is a row of source a's own 2400 tiles; later entries are 0. Over all sources a and k < send_count[a, d], dest_slot[a, d, k] names every slot of patch d exactly once; later entries are 0. send_count[a, d] is nonzero only where d's patch row equals a's px index or is one less; it is a multiple of 4, and reaches 384 in every draw. Summed over the sources a whose px index is one more than d's patch row, it is exactly 512.
All inputs are finite; a program needn't handle non-finite values.
Results may differ from a plain program's by a relative error of at most 0.0065.
Values may be sent and summed in bfloat16 or wider, within the bound.
A program may use at most 64 MiB of HBM per device.

v0:
```python
import math

import jax
import jax.numpy as jnp
from jax import lax
from jax.sharding import PartitionSpec as P

PATCH_ROWS = 512
PATCH_COLS = 512


def shifted(shard, axis, by):
    size = lax.axis_size(axis)
    pairs = [(i, i + by) for i in range(size) if 0 <= i + by < size]
    return lax.ppermute(shard, axis, pairs)


def padded(block, sides, width):
    for axis, dim in sides:
        count = lax.axis_size(axis)
        forward = [(i, i + 1) for i in range(count - 1)]
        backward = [(target, source) for source, target in forward]
        low = lax.ppermute(
            lax.slice_in_dim(block, block.shape[dim] - width, None, axis=dim), axis, forward
        )
        high = lax.ppermute(lax.slice_in_dim(block, 0, width, axis=dim), axis, backward)
        block = jnp.concatenate([low, block, high], axis=dim)
    return block


def dft_tables(length):
    positions = jnp.arange(length, dtype=jnp.int32)
    phases = positions[:, None] * positions[None, :] % length
    angles = phases.astype(jnp.float32) * (2.0 * math.pi / length)
    return (jnp.cos(angles), jnp.sin(angles))


def wavenumbers(length):
    positions = jnp.arange(length, dtype=jnp.int32)
    signed = positions - length * (positions >= (length + 1) // 2).astype(jnp.int32)
    return signed.astype(jnp.float32) * (2.0 / length)


def flexion_fields(pixels):
    row_count = pixels.shape[0]
    col_count = pixels.shape[1]
    cos_cols, sin_cols = dft_tables(col_count)
    cos_rows, sin_rows = dft_tables(row_count)
    forward_cols = jnp.concatenate([cos_cols, sin_cols], axis=1).astype(jnp.bfloat16)
    halves = jnp.dot(pixels, forward_cols, preferred_element_type=jnp.float32)
    stacked = jnp.concatenate([halves[:, :col_count], halves[:, col_count:]], axis=0).astype(
        jnp.bfloat16
    )
    forward_rows = jnp.concatenate(
        [
            jnp.concatenate([cos_rows, -sin_rows], axis=1),
            jnp.concatenate([-sin_rows, -cos_rows], axis=1),
        ],
        axis=0,
    ).astype(jnp.bfloat16)
    spectrum = jnp.dot(forward_rows, stacked, preferred_element_type=jnp.float32)
    real_part = spectrum[:row_count]
    imag_part = spectrum[row_count:]
    across = wavenumbers(col_count)[None, :]
    down = wavenumbers(row_count)[:, None]
    scale = 1.0 / (row_count * col_count)
    power = across * across + down * down
    safe_power = jnp.where(power > 0, power, 1.0)
    cube_real = across * across * across - 3.0 * across * down * down
    cube_imag = 3.0 * across * across * down - down * down * down
    one_real = (-down * real_part - across * imag_part) * scale
    one_imag = (across * real_part - down * imag_part) * scale
    kernel_real = -cube_imag / safe_power
    kernel_imag = cube_real / safe_power
    three_real = (kernel_real * real_part - kernel_imag * imag_part) * scale
    three_imag = (kernel_real * imag_part + kernel_imag * real_part) * scale
    spectra = jnp.concatenate(
        [
            jnp.concatenate([one_real, three_real], axis=1),
            jnp.concatenate([one_imag, three_imag], axis=1),
        ],
        axis=0,
    ).astype(jnp.bfloat16)
    inverse_rows = jnp.concatenate(
        [
            jnp.concatenate([cos_rows, -sin_rows], axis=1),
            jnp.concatenate([sin_rows, cos_rows], axis=1),
        ],
        axis=0,
    ).astype(jnp.bfloat16)
    columns_done = jnp.dot(inverse_rows, spectra, preferred_element_type=jnp.float32).astype(
        jnp.bfloat16
    )
    arranged = jnp.concatenate(
        [
            jnp.concatenate(
                [columns_done[:row_count, :col_count], columns_done[row_count:, :col_count]], axis=1
            ),
            jnp.concatenate(
                [columns_done[:row_count, col_count:], columns_done[row_count:, col_count:]], axis=1
            ),
        ],
        axis=0,
    )
    inverse_cols = jnp.concatenate(
        [
            jnp.concatenate([cos_cols, sin_cols], axis=1),
            jnp.concatenate([-sin_cols, cos_cols], axis=1),
        ],
        axis=0,
    ).astype(jnp.bfloat16)
    result = jnp.dot(arranged, inverse_cols, preferred_element_type=jnp.float32)
    return jnp.stack(
        [
            result[:row_count, :col_count],
            result[:row_count, col_count:],
            result[row_count:, :col_count],
            result[row_count:, col_count:],
        ]
    ).astype(jnp.bfloat16)


def blend_edges(extended, has_top, has_bottom, has_left, has_right, width):
    values = extended.astype(jnp.float32)
    row_count = values.shape[1] - 2 * width
    col_count = values.shape[2] - 2 * width
    ramp = (jnp.arange(width, dtype=jnp.float32) + 0.5) / width
    top_weight = jnp.where(has_top, ramp, 1.0)[None, :, None]
    bottom_weight = jnp.where(has_bottom, ramp[::-1], 1.0)[None, :, None]
    middle = values[:, width : width + row_count, :]
    top_band = top_weight * middle[:, :width] + (1.0 - top_weight) * values[:, :width]
    bottom_band = (
        bottom_weight * middle[:, row_count - width :]
        + (1.0 - bottom_weight) * values[:, row_count + width :]
    )
    middle = jnp.concatenate([top_band, middle[:, width : row_count - width], bottom_band], axis=1)
    left_weight = jnp.where(has_left, ramp, 1.0)[None, None, :]
    right_weight = jnp.where(has_right, ramp[::-1], 1.0)[None, None, :]
    inner = middle[:, :, width : width + col_count]
    left_band = left_weight * inner[:, :, :width] + (1.0 - left_weight) * middle[:, :, :width]
    right_band = (
        right_weight * inner[:, :, col_count - width :]
        + (1.0 - right_weight) * middle[:, :, col_count + width :]
    )
    return jnp.concatenate([left_band, inner[:, :, width : col_count - width], right_band], axis=2)


def on_device(kappa, send_list, dest_slot, send_count):
    tile_width = kappa.shape[1]
    rows_axis = lax.axis_size("px")
    cols_axis = lax.axis_size("py")
    band_index = lax.axis_index("px")
    column_index = lax.axis_index("py")
    tile_lists = send_list[0].reshape(rows_axis, cols_axis, -1)
    slot_lists = dest_slot[0].reshape(rows_axis, cols_axis, -1)
    pair_counts = send_count[0].reshape(rows_axis, cols_axis)
    slot_depth = tile_lists.shape[2]
    upper_band = jnp.maximum(band_index - 1, 0)
    picked_lists = jnp.stack([tile_lists[band_index], tile_lists[upper_band]], axis=1)
    picked_slots = jnp.stack([slot_lists[band_index], slot_lists[upper_band]], axis=1)
    upper_counts = jnp.where(band_index > 0, pair_counts[upper_band], 0)
    picked_counts = jnp.stack([pair_counts[band_index], upper_counts], axis=1)
    live_mask = jnp.arange(slot_depth, dtype=jnp.int32)[None, None, :] < picked_counts[:, :, None]
    slot_codes = jnp.where(live_mask, picked_slots + 1, 0)
    whole_band, band_lists, band_codes = (
        lax.all_gather(kappa, "py", axis=0, tiled=True),
        lax.all_gather(picked_lists, "py", axis=0, tiled=True),
        lax.all_gather(slot_codes, "py", axis=0, tiled=True),
    )
    own_lists = band_lists.reshape(cols_axis, cols_axis, 2, slot_depth)[:, column_index]
    arrived_codes = band_codes.reshape(cols_axis, cols_axis, 2, slot_depth)[:, column_index]
    offsets = (jnp.arange(cols_axis, dtype=jnp.int32) * kappa.shape[0])[:, None, None]
    tile_values = whole_band[own_lists + offsets]
    raised_values, raised_codes = shifted((tile_values[:, 1], arrived_codes[:, 1]), "px", -1)
    all_values = jnp.concatenate(
        [tile_values[:, 0].reshape(-1, tile_width), raised_values.reshape(-1, tile_width)], axis=0
    )
    all_codes = jnp.concatenate([arrived_codes[:, 0].reshape(-1), raised_codes.reshape(-1)], axis=0)
    slot_total = PATCH_ROWS * PATCH_COLS // tile_width
    target = jnp.where(all_codes > 0, all_codes - 1, slot_total)
    patch_tiles = (
        jnp.zeros((slot_total, tile_width), kappa.dtype).at[target].set(all_values, mode="drop")
    )
    fields = flexion_fields(patch_tiles.reshape(PATCH_ROWS, PATCH_COLS))
    extended = padded(fields, (("px", 1), ("py", 2)), tile_width)
    return blend_edges(
        extended,
        band_index > 0,
        band_index < rows_axis - 1,
        column_index > 0,
        column_index < cols_axis - 1,
        tile_width,
    )


def solution(mesh):
    placed = (
        P(("px", "py"), None),
        P(("px", "py"), None, None),
        P(("px", "py"), None, None),
        P(("px", "py"), None),
    )
    return jax.shard_map(
        on_device, mesh=mesh, in_specs=placed, out_specs=P(None, "px", "py"), check_vma=False
    )
```

profile of v0, /device:TPU:9, one launch (start us, length us, event | category | flops | bytes accessed | tf_op | source)
XLA Modules:
  0.0 223.6 jit_solution(5247445937136807256)
XLA Ops:
  6.5 0.7 all-gather.2.cloned.1.call-update
  7.3 0.5 broadcast.420
  7.8 1.3 reduce.3
  9.1 0.1 reshape_squeeze.13
  9.2 0.8 dynamic-slice_bitcast_fusion.1
  10.1 23.2 %all_gather.9 = s32[64,2,384]{2,0,1:T(8,128)S(1)} all-gather(s32[8,2,384]{2,0,1:T(8,128)S(1)} %fusion.57), channel_id=1, replica_groups=mesh['px'=4,'py'=8] {'py'}, dimensions={0}, use_global_device_ids=true | all-gather | bytes 221184 | tf_op jit(solution)/shard_map/all_gather | solution.py:168
  33.3 8.3 %collective-permute-start = (s32[8,384]{1,0:T(8,128)S(1)}, s32[8,384]{1,0:T(8,128)S(1)}, u32[]{:S(2)}, u32[]{:S(2)}) collective-permute-start(s32[8,384]{1,0:T(8,128)S(1)} %get-tuple-element.41), channel_id=1, source_target_pairs={{8,0},{16,8},{24,16},{9,1},{17,9},{25,17},{10,2},{18,10},{26,18},{... | collective-permute-start | bytes 36872 | tf_op jit(solution)/shard_map/ppermute | solution.py:15
  41.6 26.4 %all_gather.11 = s32[64,2,384]{2,0,1:T(8,128)S(1)} all-gather(s32[8,2,384]{2,0,1:T(8,128)S(1)} %pad_add_fusion), channel_id=1, replica_groups=mesh['px'=4,'py'=8] {'py'}, dimensions={0}, use_global_device_ids=true | all-gather | bytes 221184 | tf_op jit(solution)/shard_map/all_gather | solution.py:167
  68.0 0.1 compare_select_fusion.3
  68.2 4.0 %fusion.54 = bf16[512,512]{1,0:T(8,128)(2,1)S(1)} fusion(), kind=kLoop, calls=%fused_computation.93 | loop fusion | flops 4194304 | bytes 524288 | tf_op jit(solution)/shard_map/neg | solution.py:86
  72.2 4.3 %fusion.50 = (bf16[512,512]{1,0:T(8,128)(2,1)S(1)}, bf16[512,512]{1,0:T(8,128)(2,1)S(1)}) fusion(), kind=kLoop, calls=%fused_computation.89 | loop fusion | flops 4194304 | bytes 1048576 | tf_op jit(solution)/shard_map/sin | solution.py:35
  76.5 5.0 %negate_convert_fusion = (bf16[512,512]{1,0:T(8,128)(2,1)}, bf16[512,512]{1,0:T(8,128)(2,1)}) fusion(), kind=kLoop, calls=%fused_computation.70 | loop fusion | flops 4718592 | bytes 1048576 | tf_op jit(solution)/shard_map/convert.29
  81.5 5.0 %fusion.52 = (bf16[512,512]{1,0:T(8,128)(2,1)}, bf16[512,512]{1,0:T(8,128)(2,1)}) fusion(), kind=kLoop, calls=%fused_computation.91 | loop fusion | flops 4194304 | bytes 1048576 | tf_op jit(solution)/shard_map/convert.33
  86.5 1.2 fusion.2
  87.8 7.7 %all-gather.2.cloned.1.call-done = bf16[19200,128]{1,0:T(8,128)(2,1)} async-done(((bf16[2400,128]{1,0:T(8,128)(2,1)}), bf16[19200,128]{1,0:T(8,128)(2,1)}) %all-gather.2.cloned.1.call-update) | async-done | bytes 4915216 | tf_op jit(solution)/shard_map/all_gather | solution.py:166
  95.5 19.5 %gather_fusion = bf16[6144,128]{1,0:T(8,128)(2,1)S(1)} fusion(bf16[19200,128]{1,0:T(8,128)(2,1)} %all-gather.2.cloned.1.call-done, s32[6144]{0:T(1024)S(1)} %broadcast_clamp_fusion), kind=kCustom, calls=%fused_computation | custom fusion | bytes 3170304 | tf_op jit(solution)/shard_map/gather | solution.py:173
  115.0 0.1 fusion.71
  115.1 3.4 %collective-permute-start.1 = (bf16[8,384,128]{2,1,0:T(8,128)(2,1)S(1)}, bf16[8,384,128]{2,1,0:T(8,128)(2,1)S(1)}, u32[]{:S(2)}, u32[]{:S(2)}) collective-permute-start(bf16[8,384,128]{2,1,0:T(8,128)(2,1)S(1)} %get-tuple-element.32), channel_id=1, source_target_pairs={{8,0},{16,8},{24,16},{9,1},{17,9},{25,17},{10,2},{18,10},{26,18},{... | collective-permute-start | bytes 2359304 | tf_op jit(solution)/shard_map/ppermute | solution.py:15
  118.6 10.6 %collective-permute-done.1 = bf16[8,384,128]{2,1,0:T(8,128)(2,1)S(1)} collective-permute-done((bf16[8,384,128]{2,1,0:T(8,128)(2,1)S(1)}, bf16[8,384,128]{2,1,0:T(8,128)(2,1)S(1)}, u32[]{:S(2)}, u32[]{:S(2)}) %collective-permute-start.1) | collective-permute-done | bytes 786464 | tf_op jit(solution)/shard_map/ppermute | solution.py:15
  129.2 21.4 %scatter_custom_fusion = bf16[2048,128]{1,0:T(8,128)(2,1)S(1)} fusion(s32[6144]{0:T(1024)S(1)} %bitcast.60, bf16[3072,128]{1,0:T(8,128)(2,1)S(1)} %bitcast.54, bf16[]{:T(256)} %constant.86, bf16[3072,128]{1,0:T(8,128)(2,1)S(1)} %bitcast.53, bf16[]{:T(256)} %constant.22.clone.1), kind=kCustom, calls=%fused_computation.44 | custom fusion | flops 3145728 | bytes 2097156 | tf_op jit(solution)/shard_map/scatter | solution.py:182
  150.5 0.3 reshape.195
  150.9 0.7 convolution_convert_fusion
  151.7 0.4 copy-done
  152.1 0.1 copy-done.1
  152.2 0.2 copy-done.4
  152.4 1.3 fusion.1
  153.7 1.4 multiply_convert_fusion.3
  155.1 2.4 %fusion.29 = bf16[1024,1024]{0,1:T(8,128)(2,1)S(1)} fusion(bf16[512,512]{0,1:T(8,128)(2,1)S(1)} %get-tuple-element.19, bf16[512,512]{0,1:T(8,128)(2,1)S(1)} %get-tuple-element.18, bf16[512,512]{0,1:T(8,128)(2,1)S(1)} %get-tuple-element.20, bf16[512,512]{0,1:T(8,128)(2,1)S(1)} %get-tuple-element.17, bf16[512,1024]{1,0:T(8,128)(2,1)S(1)} %copy-done, ...), kind=kOutput, calls=%fused_computation.37 | convolution fusion | flops 2163212288 | bytes 6291456 | tf_op jit(solution)/shard_map/dot_general | solution.py:91
  157.5 0.2 fusion.70
  157.7 2.4 %fusion.24 = bf16[1024,1024]{1,0:T(8,128)(2,1)S(1)} fusion(bf16[512,512]{1,0:T(8,128)(2,1)S(1)} %copy-done.2, bf16[512,512]{1,0:T(8,128)(2,1)S(1)} %copy-done.1, bf16[512,1024]{1,0:T(8,128)(2,1)S(1)} %get-tuple-element.36, bf16[512,512]{0,1:T(8,128)(2,1)S(1)} %get-tuple-element.28, bf16[512,512]{0,1:T(8,128)(2,1)S(1)} %get-tuple-element.29, ...), kind=kOutput, calls=%fused_computation.36 | convolution fusion | flops 2163212288 | bytes 6291456 | tf_op jit(solution)/shard_map/dot_general | solution.py:112
  160.1 0.2 slice_bitcast_fusion.4
  160.4 1.9 collective-permute-start.2
  162.3 2.4 %collective-permute-start.3 = (bf16[4,128,512]{2,1,0:T(8,128)(2,1)S(1)}, bf16[4,128,512]{2,1,0:T(8,128)(2,1)S(1)}, u32[]{:S(2)}, u32[]{:S(2)}) collective-permute-start(bf16[4,128,512]{2,1,0:T(8,128)(2,1)S(1)} %get-tuple-element.22), channel_id=1, source_target_pairs={{8,0},{16,8},{24,16},{9,1},{17,9},{25,17},{10,2},{18,10},{26,18},{... | collective-permute-start | bytes 1572872 | tf_op jit(solution)/shard_map/ppermute | solution.py:26
  164.7 3.7 %collective-permute-done.2 = bf16[4,128,512]{2,1,0:T(8,128)(2,1)S(1)} collective-permute-done((bf16[4,128,512]{2,1,0:T(8,128)(2,1)S(1)}, bf16[4,128,512]{2,1,0:T(8,128)(2,1)S(1)}, u32[]{:S(2)}, u32[]{:S(2)}) %collective-permute-start.2) | collective-permute-done | bytes 524320 | tf_op jit(solution)/shard_map/ppermute | solution.py:23
  168.4 4.4 %collective-permute-done.3 = bf16[4,128,512]{2,1,0:T(8,128)(2,1)S(1)} collective-permute-done((bf16[4,128,512]{2,1,0:T(8,128)(2,1)S(1)}, bf16[4,128,512]{2,1,0:T(8,128)(2,1)S(1)}, u32[]{:S(2)}, u32[]{:S(2)}) %collective-permute-start.3) | collective-permute-done | bytes 524320 | tf_op jit(solution)/shard_map/ppermute | solution.py:26
  172.8 1.5 pad_maximum_fusion.20
  174.2 2.5 %collective-permute-start.4 = (bf16[4,768,128]{2,1,0:T(8,128)(2,1)}, bf16[4,768,128]{2,1,0:T(8,128)(2,1)}, u32[]{:S(2)}, u32[]{:S(2)}) collective-permute-start(bf16[4,768,128]{2,1,0:T(8,128)(2,1)} %get-tuple-element.13), channel_id=1, source_target_pairs={{0,1},{1,2},{2,3},{3,4},{4,5},{5,6},{6,7},{8,9},{9,10},{10,11},{11... | collective-permute-start | bytes 2359304 | tf_op jit(solution)/shard_map/ppermute | solution.py:23
  176.7 3.7 %collective-permute-start.5 = (bf16[4,768,128]{2,1,0:T(8,128)(2,1)}, bf16[4,768,128]{2,1,0:T(8,128)(2,1)}, u32[]{:S(2)}, u32[]{:S(2)}) collective-permute-start(bf16[4,768,128]{2,1,0:T(8,128)(2,1)} %get-tuple-element.14), channel_id=1, source_target_pairs={{1,0},{2,1},{3,2},{4,3},{5,4},{6,5},{7,6},{9,8},{10,9},{11,10},{12... | collective-permute-start | bytes 2359304 | tf_op jit(solution)/shard_map/ppermute | solution.py:26
  180.5 0.1 reverse.4
  180.6 25.0 %collective-permute-done.4 = bf16[4,768,128]{2,1,0:T(8,128)(2,1)} collective-permute-done((bf16[4,768,128]{2,1,0:T(8,128)(2,1)}, bf16[4,768,128]{2,1,0:T(8,128)(2,1)}, u32[]{:S(2)}, u32[]{:S(2)}) %collective-permute-start.4) | collective-permute-done | bytes 786464 | tf_op jit(solution)/shard_map/ppermute | solution.py:23
  205.5 2.4 %collective-permute-done.5 = bf16[4,768,128]{2,1,0:T(8,128)(2,1)} collective-permute-done((bf16[4,768,128]{2,1,0:T(8,128)(2,1)}, bf16[4,768,128]{2,1,0:T(8,128)(2,1)}, u32[]{:S(2)}, u32[]{:S(2)}) %collective-permute-start.5) | collective-permute-done | bytes 786464 | tf_op jit(solution)/shard_map/ppermute | solution.py:26
  208.0 4.6 %maximum_convert_fusion = f32[4,768,768]{2,1,0:T(8,128)S(1)} fusion(bf16[4,768,128]{2,1,0:T(8,128)(2,1)} %collective-permute-done.5, bf16[4,128,512]{2,1,0:T(8,128)(2,1)S(1)} %collective-permute-done.3, bf16[1,512,512]{2,1,0:T(8,128)(2,1)S(1)} %get-tuple-element.24, bf16[1,512,512]{2,1,0:T(8,128)(2,1)S(1)} %get-tuple-element.25, ...), kind=kLoop, calls=%fused_computation.3 | loop fusion | flops 37748736 | bytes 14155776 | tf_op jit(solution)/shard_map/convert_element_type | solution.py:124
  212.5 0.2 slice.154
  212.8 0.5 fusion.33
  213.3 0.6 pad_maximum_fusion
  213.9 0.1 slice.157
  214.0 0.2 fusion.42
  214.3 2.5 %pad_maximum_fusion.1 = f32[4,512,512]{2,1,0:T(8,128)} fusion(f32[4,512,128]{2,1,0:T(8,128)S(1)} %get-tuple-element.12, f32[4,512,256]{2,1,0:T(8,128)S(1)} %slice.157, f32[4,512,128]{2,1,0:T(8,128)S(1)} %get-tuple-element.11), kind=kLoop, calls=%fused_computation.4 | loop fusion | flops 2097152 | bytes 8388608 | tf_op jit(solution)/shard_map/concatenate | solution.py:145
  (35 shorter events, 0.5 us)
Async XLA Ops:
  6.5 89.0 %all-gather.2.cloned.1.call-start = ((), (), s32[]{:S(2)}) async-start(), calls=%async_computation | async-start | bytes 5529600 | tf_op jit(solution)/shard_map/all_gather | solution.py:166
  33.3 54.5 %collective-permute-start = (s32[8,384]{1,0:T(8,128)S(1)}, s32[8,384]{1,0:T(8,128)S(1)}, u32[]{:S(2)}, u32[]{:S(2)}) collective-permute-start(s32[8,384]{1,0:T(8,128)S(1)} %get-tuple-element.41), channel_id=1, source_target_pairs={{8,0},{16,8},{24,16},{9,1},{17,9},{25,17},{10,2},{18,10},{26,18},{... | collective-permute-start | bytes 36872 | tf_op jit(solution)/shard_map/ppermute | solution.py:15
  115.1 14.1 %collective-permute-start.1 = (bf16[8,384,128]{2,1,0:T(8,128)(2,1)S(1)}, bf16[8,384,128]{2,1,0:T(8,128)(2,1)S(1)}, u32[]{:S(2)}, u32[]{:S(2)}) collective-permute-start(bf16[8,384,128]{2,1,0:T(8,128)(2,1)S(1)} %get-tuple-element.32), channel_id=1, source_target_pairs={{8,0},{16,8},{24,16},{9,1},{17,9},{25,17},{10,2},{18,10},{26,18},{... | collective-permute-start | bytes 2359304 | tf_op jit(solution)/shard_map/ppermute | solution.py:15
  150.9 1.2 copy-start
  150.9 1.3 copy-start.1
  150.9 1.5 copy-start.4
  153.7 1.4 copy-start.2
  153.7 1.4 copy-start.3
  160.4 8.0 %collective-permute-start.2 = (bf16[4,128,512]{2,1,0:T(8,128)(2,1)S(1)}, bf16[4,128,512]{2,1,0:T(8,128)(2,1)S(1)}, u32[]{:S(2)}, u32[]{:S(2)}) collective-permute-start(bf16[4,128,512]{2,1,0:T(8,128)(2,1)S(1)} %get-tuple-element.21), channel_id=1, source_target_pairs={{0,8},{8,16},{16,24},{1,9},{9,17},{17,25},{2,10},{10,18},{18,26},{... | collective-permute-start | bytes 1572872 | tf_op jit(solution)/shard_map/ppermute | solution.py:23
  162.3 10.5 %collective-permute-start.3 = (bf16[4,128,512]{2,1,0:T(8,128)(2,1)S(1)}, bf16[4,128,512]{2,1,0:T(8,128)(2,1)S(1)}, u32[]{:S(2)}, u32[]{:S(2)}) collective-permute-start(bf16[4,128,512]{2,1,0:T(8,128)(2,1)S(1)} %get-tuple-element.22), channel_id=1, source_target_pairs={{8,0},{16,8},{24,16},{9,1},{17,9},{25,17},{10,2},{18,10},{26,18},{... | collective-permute-start | bytes 1572872 | tf_op jit(solution)/shard_map/ppermute | solution.py:26
  174.2 31.3 %collective-permute-start.4 = (bf16[4,768,128]{2,1,0:T(8,128)(2,1)}, bf16[4,768,128]{2,1,0:T(8,128)(2,1)}, u32[]{:S(2)}, u32[]{:S(2)}) collective-permute-start(bf16[4,768,128]{2,1,0:T(8,128)(2,1)} %get-tuple-element.13), channel_id=1, source_target_pairs={{0,1},{1,2},{2,3},{3,4},{4,5},{5,6},{6,7},{8,9},{9,10},{10,11},{11... | collective-permute-start | bytes 2359304 | tf_op jit(solution)/shard_map/ppermute | solution.py:23
  176.7 31.2 %collective-permute-start.5 = (bf16[4,768,128]{2,1,0:T(8,128)(2,1)}, bf16[4,768,128]{2,1,0:T(8,128)(2,1)}, u32[]{:S(2)}, u32[]{:S(2)}) collective-permute-start(bf16[4,768,128]{2,1,0:T(8,128)(2,1)} %get-tuple-element.14), channel_id=1, source_target_pairs={{1,0},{2,1},{3,2},{4,3},{5,4},{6,5},{7,6},{9,8},{10,9},{11,10},{12... | collective-permute-start | bytes 2359304 | tf_op jit(solution)/shard_map/ppermute | solution.py:26
Sparse Core Ops, SparseCore 0:
  9.5 85.9 all-gather.1
where the time goes:
time: 224 us
  waiting for transfers between devices  54.4 us (24%)
  other arithmetic  53.8 us (24%)
  blocking collectives  49.6 us (22%)
  local copies, waits for them, and re-layouts  23 us (10%)
  starting transfers between devices  22.2 us (10%)
  between operations  13.8 us (6%)
  matrix products  6.84 us (3%)
    ppermute x2, waiting for transfers between devices, padded(): lax.ppermute(lax.slice_in_dim(block, block.shape[dim] - width, None, axis...  28.6 us
    all_gather x1, blocking collectives, on_device(): lax.all_gather(picked_lists, 'py', axis=0, tiled=True)  26.4 us
    all_gather x1, blocking collectives, on_device(): lax.all_gather(slot_codes, 'py', axis=0, tiled=True)  23.2 us
    scatter x1, other arithmetic, on_device(): jnp.zeros((slot_total, tile_width), kappa.dtype).at[target]  21.4 us
    gather x1, local copies, waits for them, and re-layouts, on_device(): tile_values = whole_band[own_lists + offsets]  19.5 us
    another operation x4, other arithmetic  12.6 us
    ppermute x2, starting transfers between devices, shifted(): return lax.ppermute(shard, axis, pairs)  11.7 us
    ppermute x2, waiting for transfers between devices, shifted(): return lax.ppermute(shard, axis, pairs)  10.6 us
  transfers between devices with their start and end apart: 7, of which 6 were waited for; matrix products, arithmetic and copies ran while one was open for 10% of the time, Pallas kernels for 0%

commit v1 on v0

v1 whole, which is shorter than its diff:
```python
import functools
import math

import jax
import jax.numpy as jnp
import numpy as np
from jax import lax
from jax.experimental import pallas as pl
from jax.experimental.pallas import tpu as pltpu
from jax.sharding import PartitionSpec as P

PATCH = 512
MESH = pl.DeviceIdType.MESH
STEP = 16


def gather_kernel(n_px, n_py, kappa_ref, list_ref, count_ref, slot_ref, tiles_ref, aux_ref, wide, stage):
    i = lax.axis_index("px")
    j = lax.axis_index("py")
    cap = list_ref.shape[2]
    width = aux_ref.shape[3]
    wide[...] = kappa_ref[...].astype(jnp.float32)
    lanes = lax.broadcasted_iota(jnp.int32, (1, cap), 1)
    dump = PATCH * PATCH // kappa_ref.shape[1]

    def one(t, carry):
        b = t // n_py
        o = lax.rem(t, n_py)
        row = jnp.maximum(i - b, 0)
        d = row * n_py + lax.rem(j + o, n_py)
        count = jnp.where(i - b >= 0, count_ref[0, d], 0)

        def rows(c, carry):
            base = pl.multiple_of(c * STEP, STEP)
            for k in range(STEP):
                source = list_ref[0, d, base + k]
                stage[pl.ds(base + k, 1), :] = wide[pl.ds(source, 1), :]
            return carry

        lax.fori_loop(0, (count + STEP - 1) // STEP, rows, 0)
        tiles_ref[b, o] = stage[...].astype(jnp.bfloat16)
        slots = slot_ref[0, pl.ds(d, 1), :]
        aux_ref[b, o] = jnp.full((1, width), count, jnp.int32)
        aux_ref[b, o, :, :cap] = jnp.where(lanes < count, slots, dump)
        return carry

    lax.fori_loop(0, 2 * n_py, one, 0)


def gather_tiles(n_px, n_py, kappa, send_list, dest_slot, send_count):
    cap = send_list.shape[2]
    width = (cap + 128) // 128 * 128
    vmem = pl.BlockSpec(memory_space=pltpu.VMEM)
    smem = pl.BlockSpec(memory_space=pltpu.SMEM)
    return pl.pallas_call(
        functools.partial(gather_kernel, n_px, n_py),
        out_shape=(
            jax.ShapeDtypeStruct((2, n_py, cap, kappa.shape[1]), jnp.bfloat16),
            jax.ShapeDtypeStruct((2, n_py, 1, width), jnp.int32),
        ),
        in_specs=[vmem, smem, smem, vmem],
        out_specs=(vmem, vmem),
        scratch_shapes=[
            pltpu.VMEM(kappa.shape, jnp.float32),
            pltpu.VMEM((cap, kappa.shape[1]), jnp.float32),
        ],
        compiler_params=pltpu.CompilerParams(vmem_limit_bytes=32 * 2**20),
        name="gather_tiles",
    )(kappa, send_list, send_count, dest_slot)


def exchange_kernel(n_px, n_py, tiles, aux, got_tiles, got_aux, send_t, recv_t, send_a, recv_a, local):
    i = lax.axis_index("px")
    j = lax.axis_index("py")
    has_up = i > 0
    has_down = i < n_px - 1
    barrier = pltpu.get_barrier_semaphore()
    for o in range(1, n_py):
        pl.semaphore_signal(barrier, inc=1, device_id=(i, lax.rem(j + o, n_py)), device_id_type=MESH)

    @pl.when(has_down)
    def _():
        for o in range(n_py):
            pl.semaphore_signal(
                barrier, inc=1, device_id=(i + 1, lax.rem(j + o, n_py)), device_id_type=MESH
            )

    pl.semaphore_wait(barrier, n_py - 1 + jnp.where(has_up, n_py, 0))

    def copies(b, o):
        target = (i - b, lax.rem(j + o, n_py))
        return [
            pltpu.make_async_remote_copy(
                src_ref=source.at[b, o],
                dst_ref=landing.at[b, o],
                send_sem=send.at[b, o],
                recv_sem=recv.at[b, o],
                device_id=target,
                device_id_type=MESH,
            )
            for source, landing, send, recv in (
                (tiles, got_tiles, send_t, recv_t),
                (aux, got_aux, send_a, recv_a),
            )
        ]

    own = [
        pltpu.make_async_copy(tiles.at[0, 0], got_tiles.at[0, 0], local.at[0]),
        pltpu.make_async_copy(aux.at[0, 0], got_aux.at[0, 0], local.at[1]),
    ]
    for copy in own:
        copy.start()
    order = sorted(range(n_py), key=lambda o: -min(o, n_py - o))
    for o in order:
        if o > 0:
            for copy in copies(0, o):
                copy.start()

        @pl.when(has_up)
        def _():
            for copy in copies(1, o):
                copy.start()

    for o in order:
        if o > 0:
            for copy in copies(0, o):
                copy.wait()

        @pl.when(has_up)
        def _():
            for copy in copies(1, o):
                copy.wait_send()

        @pl.when(has_down)
        def _():
            for copy in copies(1, o):
                copy.wait_recv()

    for copy in own:
        copy.wait()


def exchange(n_px, n_py, tiles, aux):
    anywhere = pl.BlockSpec(memory_space=pl.ANY)
    return pl.pallas_call(
        functools.partial(exchange_kernel, n_px, n_py),
        out_shape=(
            jax.ShapeDtypeStruct(tiles.shape, tiles.dtype),
            jax.ShapeDtypeStruct(aux.shape, aux.dtype),
        ),
        in_specs=[anywhere] * 2,
        out_specs=(anywhere, anywhere),
        scratch_shapes=[pltpu.SemaphoreType.DMA((2, n_py))] * 4 + [pltpu.SemaphoreType.DMA((2,))],
        compiler_params=pltpu.CompilerParams(collective_id=0, has_side_effects=True),
        name="exchange_tiles",
    )(tiles, aux)


def place_kernel(n_px, n_py, tiles_ref, aux_ref, image_ref, wide, patch):
    i = lax.axis_index("px")
    cap = tiles_ref.shape[2]
    per_row = PATCH // tiles_ref.shape[3]
    tile = tiles_ref.shape[3]

    def one(t, carry):
        b = t // n_py
        o = lax.rem(t, n_py)
        live = jnp.logical_or(b == 0, i < n_px - 1)

        @pl.when(live)
        def _():
            wide[...] = tiles_ref[b, o].astype(jnp.float32)

            def rows(c, carry):
                base = pl.multiple_of(c * STEP, STEP)
                for k in range(STEP):
                    slot = aux_ref[b, o, 0, base + k]
                    patch[pl.ds(slot, 1), :] = wide[pl.ds(base + k, 1), :]
                return carry

            lax.fori_loop(0, (aux_ref[b, o, 0, cap] + STEP - 1) // STEP, rows, 0)

        return carry

    lax.fori_loop(0, 2 * n_py, one, 0)
    for c in range(per_row):
        image_ref[:, c * tile : (c + 1) * tile] = patch[
            pl.ds(c, PATCH, stride=per_row), :
        ].astype(jnp.bfloat16)


def place_tiles(n_px, n_py, tiles, aux):
    vmem = pl.BlockSpec(memory_space=pltpu.VMEM)
    smem = pl.BlockSpec(memory_space=pltpu.SMEM)
    tile = tiles.shape[3]
    return pl.pallas_call(
        functools.partial(place_kernel, n_px, n_py),
        out_shape=jax.ShapeDtypeStruct((PATCH, PATCH), jnp.bfloat16),
        in_specs=[vmem, smem],
        out_specs=vmem,
        scratch_shapes=[
            pltpu.VMEM((tiles.shape[2], tile), jnp.float32),
            pltpu.VMEM((PATCH * PATCH // tile + 8, tile), jnp.float32),
        ],
        compiler_params=pltpu.CompilerParams(vmem_limit_bytes=32 * 2**20),
        name="place_tiles",
    )(tiles, aux)


def dft_tables(length):
    positions = np.arange(length)
    angles = (positions[:, None] * positions[None, :] % length).astype(np.float32) * np.float32(
        2.0 * math.pi / length
    )
    return np.cos(angles).astype(np.float32), np.sin(angles).astype(np.float32)


def wavenumbers(length):
    positions = np.arange(length)
    return (positions - length * (positions >= (length + 1) // 2)).astype(np.float32) * np.float32(2.0 / length)


def flexion_fields(pixels):
    n = pixels.shape[0]
    cos, sin = dft_tables(n)
    bf16 = jnp.bfloat16
    halves = jnp.dot(pixels, jnp.asarray(np.concatenate([cos, sin], 1), bf16), preferred_element_type=jnp.float32)
    stacked = jnp.concatenate([halves[:, :n], halves[:, n:]], axis=0).astype(bf16)
    forward = np.block([[cos, -sin], [-sin, -cos]])
    spectrum = jnp.dot(jnp.asarray(forward, bf16), stacked, preferred_element_type=jnp.float32)
    real_part, imag_part = spectrum[:n], spectrum[n:]
    across = wavenumbers(n)[None, :]
    down = wavenumbers(n)[:, None]
    scale = np.float32(1.0 / (n * n))
    power = across * across + down * down
    safe = np.where(power > 0, power, 1.0).astype(np.float32)
    kernel_real = jnp.asarray(-(3.0 * across * across * down - down * down * down) / safe, jnp.float32)
    kernel_imag = jnp.asarray((across * across * across - 3.0 * across * down * down) / safe, jnp.float32)
    across, down = jnp.asarray(across), jnp.asarray(down)
    one_real = (-down * real_part - across * imag_part) * scale
    one_imag = (across * real_part - down * imag_part) * scale
    three_real = (kernel_real * real_part - kernel_imag * imag_part) * scale
    three_imag = (kernel_real * imag_part + kernel_imag * real_part) * scale
    spectra = jnp.concatenate(
        [jnp.concatenate([one_real, three_real], 1), jnp.concatenate([one_imag, three_imag], 1)], 0
    ).astype(bf16)
    inverse = np.block([[cos, -sin], [sin, cos]])
    done = jnp.dot(jnp.asarray(inverse, bf16), spectra, preferred_element_type=jnp.float32).astype(bf16)
    arranged = jnp.concatenate(
        [
            jnp.concatenate([done[:n, :n], done[n:, :n]], 1),
            jnp.concatenate([done[:n, n:], done[n:, n:]], 1),
        ],
        0,
    )
    inverse_cols = np.block([[cos, sin], [-sin, cos]])
    result = jnp.dot(arranged, jnp.asarray(inverse_cols, bf16), preferred_element_type=jnp.float32)
    return jnp.stack([result[:n, :n], result[:n, n:], result[n:, :n], result[n:, n:]]).astype(bf16)


def neighbours(low, high, axis):
    count = lax.axis_size(axis)
    forward = [(k, k + 1) for k in range(count - 1)]
    backward = [(k + 1, k) for k in range(count - 1)]
    return lax.ppermute(high, axis, forward), lax.ppermute(low, axis, backward)


def blend_axis(values, axis, dim, width):
    size = values.shape[dim]
    index = lax.axis_index(axis)
    ramp = (np.arange(width, dtype=np.float32) + np.float32(0.5)) / np.float32(width)
    shape = [1, 1, 1]
    shape[dim] = width
    first = jnp.where(index > 0, ramp, 1.0).reshape(shape)
    last = jnp.where(index < lax.axis_size(axis) - 1, ramp[::-1], 1.0).reshape(shape)
    low = lax.slice_in_dim(values, 0, width, axis=dim)
    high = lax.slice_in_dim(values, size - width, size, axis=dim)
    before, after = neighbours(low.astype(jnp.bfloat16), high.astype(jnp.bfloat16), axis)
    low = first * low.astype(jnp.float32) + (1.0 - first) * before.astype(jnp.float32)
    high = last * high.astype(jnp.float32) + (1.0 - last) * after.astype(jnp.float32)
    middle = lax.slice_in_dim(values, width, size - width, axis=dim).astype(jnp.float32)
    return jnp.concatenate([low, middle, high], axis=dim)


def on_device(kappa, send_list, dest_slot, send_count):
    n_px = lax.axis_size("px")
    n_py = lax.axis_size("py")
    tiles, aux = gather_tiles(n_px, n_py, kappa, send_list, dest_slot, send_count)
    tiles, aux = exchange(n_px, n_py, tiles, aux)
    pixels = place_tiles(n_px, n_py, tiles, aux)
    fields = flexion_fields(pixels)
    rows = blend_axis(fields, "px", 1, kappa.shape[1])
    return blend_axis(rows, "py", 2, kappa.shape[1])


def solution(mesh):
    placed = (
        P(("px", "py"), None),
        P(("px", "py"), None, None),
        P(("px", "py"), None, None),
        P(("px", "py"), None),
    )
    return jax.shard_map(
        on_device, mesh=mesh, in_specs=placed, out_specs=P(None, "px", "py"), check_vma=False
    )
```

time: 224 us -> 135 us (0.60)
  the two profiles are of different devices: /device:TPU:9 before, /device:TPU:14 now
where the time goes in v1:
time: 135 us; the launch traced here: 133 us
  Pallas kernels  57.9 us (43%)
  waiting for transfers between devices  38.5 us (29%)
  local copies, waits for them, and re-layouts  11.9 us (9%)
  starting transfers between devices  9.15 us (7%)
  matrix products  8.44 us (6%)
  other arithmetic  7.03 us (5%)
    pallas_call x1, Pallas kernels, exchange(): pl.pallas_call(functools.partial(exchange_kernel, n_px, n_py), out_shape=...  43.8 us
    ppermute x2, waiting for transfers between devices, neighbours(): lax.ppermute(high, axis, forward)  22.2 us
    ppermute x2, waiting for transfers between devices, neighbours(): lax.ppermute(low, axis, backward)  16.4 us
    unnamed x40, local copies, waits for them, and re-layouts  11.6 us
    pallas_call x1, Pallas kernels, place_tiles(): pl.pallas_call(functools.partial(place_kernel, n_px, n_py), out_shape=jax...  7.2 us
    pallas_call x1, Pallas kernels, gather_tiles(): pl.pallas_call(functools.partial(gather_kernel, n_px, n_py), out_shape=(j...  6.91 us
    ppermute x2, starting transfers between devices, neighbours(): lax.ppermute(high, axis, forward)  5.32 us
    ppermute x2, starting transfers between devices, neighbours(): lax.ppermute(low, axis, backward)  3.83 us
  transfers between devices with their start and end apart: 4, of which 4 were waited for; matrix products, arithmetic and copies ran while one was open for 0% of the time, Pallas kernels for 0%

profile of v1, /device:TPU:14, one launch (start us, length us, event | category | flops | bytes accessed | tf_op | source)
XLA Modules:
  0.0 133.3 jit_solution(10256782515660519556)
XLA Ops:
  0.0 1.1 copy-done.2
  1.1 0.8 copy-done.3
  1.9 0.8 copy-done.4
  2.7 0.7 copy-done.7
  3.3 6.9 %gather_tiles.1 = (bf16[2,8,384,128]{3,2,1,0:T(8,128)(2,1)S(1)}, s32[2,8,1,512]{3,2,1,0:T(1,128)S(1)}) custom-call(bf16[2400,128]{1,0:T(8,128)(2,1)S(1)} %copy-done.2, s32[1,32,384]{2,1,0:T(8,128)S(1)} %copy-done.3, s32[1,32]{1,0:T(1,128)S(1)} %copy-done.7, s32[1,32,384]{2,1,0:T(8,128)S(1)} %copy-done.4), custom_call_target="tpu_custom_call" | custom-call | tf_op jit(solution)/shard_map/gather_tiles/pallas_call | solution.py:55
  10.2 0.0 copy-start
  10.3 1.1 copy-done
  11.4 0.6 copy-done.6
  12.0 43.8 %exchange_tiles.1 = (bf16[2,8,384,128]{3,2,1,0:T(8,128)(2,1)}, s32[2,8,1,512]{3,2,1,0:T(1,128)}) custom-call(bf16[2,8,384,128]{3,2,1,0:T(8,128)(2,1)} %copy-done, s32[2,8,1,512]{3,2,1,0:T(1,128)} %copy-done.6), custom_call_target="tpu_custom_call" | custom-call | tf_op jit(solution)/shard_map/exchange_tiles/pallas_call | solution.py:145
  55.8 0.0 copy-start.1
  55.9 1.4 %copy-done.1 = bf16[2,8,384,128]{3,2,1,0:T(8,128)(2,1)S(1)} copy-done((bf16[2,8,384,128]{3,2,1,0:T(8,128)(2,1)S(1)}, bf16[2,8,384,128]{3,2,1,0:T(8,128)(2,1)}, u32[]{:S(2)}) %copy-start.1) | copy-done | bytes 1572888
  57.3 0.8 copy-done.5
  58.0 7.2 %place_tiles.1 = bf16[512,512]{1,0:T(8,128)(2,1)S(1)} custom-call(bf16[2,8,384,128]{3,2,1,0:T(8,128)(2,1)S(1)} %copy-done.1, s32[2,8,1,512]{3,2,1,0:T(1,128)S(1)} %copy-done.5), custom_call_target="tpu_custom_call" | custom-call | tf_op jit(solution)/shard_map/place_tiles/pallas_call | solution.py:196
  65.2 1.9 %convolution_convert_fusion = bf16[512,1024]{1,0:T(8,128)(2,1)S(1)} fusion(bf16[512,512]{1,0:T(8,128)(2,1)S(1)} %place_tiles.1, bf16[512,1024]{1,0:T(8,128)(2,1)} %constant.40.clone), kind=kOutput, calls=%fused_computation.19 | convolution fusion | flops 537395200 | bytes 2621440 | tf_op jit(solution)/shard_map/dot_general | solution.py:227
  67.2 0.0 copy-start.11
  67.2 0.8 fusion.24
  68.0 0.5 copy-done.11
  68.4 0.8 add_bitcast_fusion
  69.2 0.4 copy-done.8
  69.6 0.3 copy-done.9
  70.0 0.6 multiply_convert_fusion.1
  70.6 0.6 copy-done.19
  71.2 1.3 fusion.16
  72.5 1.3 fusion.14
  73.8 0.0 copy-start.18
  73.8 0.2 fusion.30
  74.0 1.4 %copy-done.18 = bf16[1024,1024]{1,0:T(8,128)(2,1)S(1)} copy-done((bf16[1024,1024]{1,0:T(8,128)(2,1)S(1)}, bf16[1024,1024]{1,0:T(8,128)(2,1)}, u32[]{:S(2)}) %copy-start.18) | copy-done | bytes 2097176
  75.4 2.4 %fusion.11 = bf16[1024,1024]{1,0:T(8,128)(2,1)S(1)} fusion(bf16[1024,1024]{1,0:T(8,128)(2,1)S(1)} %copy-done.18, bf16[512,512]{0,1:T(8,128)(2,1)S(1)} %get-tuple-element.28, bf16[512,512]{0,1:T(8,128)(2,1)S(1)} %get-tuple-element.29, bf16[512,512]{0,1:T(8,128)(2,1)S(1)} %get-tuple-element.30, bf16[512,512]{0,1:T(8,128)(2,1)S(1)} %get-tuple-element.27), kind=kOutput, calls=%fused_computation.17 | convolution fusion | flops 2156920832 | bytes 6291456 | tf_op jit(solution)/shard_map/dot_general | solution.py:257
  77.8 0.2 slice_bitcast_fusion.3
  77.9 0.0 copy-start.17
  78.0 1.9 %collective-permute-start = (bf16[4,128,512]{2,1,0:T(8,128)(2,1)S(1)}, bf16[4,128,512]{2,1,0:T(8,128)(2,1)S(1)}, u32[]{:S(2)}, u32[]{:S(2)}) collective-permute-start(bf16[4,128,512]{2,1,0:T(8,128)(2,1)S(1)} %pad_maximum_fusion.5), channel_id=1, source_target_pairs={{0,8},{8,16},{16,24},{1,9},{9,17},{17,25},{2,10},{10,18},{18,26},{... | collective-permute-start | bytes 1572872 | tf_op jit(solution)/shard_map/ppermute | solution.py:265
  80.0 8.9 %collective-permute-done = bf16[4,128,512]{2,1,0:T(8,128)(2,1)S(1)} collective-permute-done((bf16[4,128,512]{2,1,0:T(8,128)(2,1)S(1)}, bf16[4,128,512]{2,1,0:T(8,128)(2,1)S(1)}, u32[]{:S(2)}, u32[]{:S(2)}) %collective-permute-start) | collective-permute-done | bytes 524320 | tf_op jit(solution)/shard_map/ppermute | solution.py:265
  88.9 0.8 copy-done.13
  89.7 2.1 %multiply_add_fusion.3 = (f32[4,128,512]{2,1,0:T(8,128)S(1)}, bf16[4,128,512]{2,1,0:T(8,128)(2,1)}) fusion(bf16[4,128,512]{2,1,0:T(8,128)(2,1)} %copy-done.13, f32[128]{0:T(128)S(1)} %get-tuple-element.38, f32[128]{0:T(128)S(1)} %get-tuple-element.40, bf16[1,512,512]{2,1,0:T(8,128)(2,1)S(1)} %get-tuple-element.24, ...), kind=kLoop, calls=%fused_computation.36 | loop fusion | flops 3407872 | bytes 4195328 | tf_op jit(solution)/shard_map/add | solution.py:279
  91.7 1.9 %collective-permute-start.1 = (bf16[4,128,512]{2,1,0:T(8,128)(2,1)}, bf16[4,128,512]{2,1,0:T(8,128)(2,1)}, u32[]{:S(2)}, u32[]{:S(2)}) collective-permute-start(bf16[4,128,512]{2,1,0:T(8,128)(2,1)} %get-tuple-element.18), channel_id=1, source_target_pairs={{8,0},{16,8},{24,16},{9,1},{17,9},{25,17},{10,2},{18,10},{26,18},{... | collective-permute-start | bytes 1572872 | tf_op jit(solution)/shard_map/ppermute | solution.py:265
  93.6 0.0 copy-start.16
  93.7 0.3 fusion.15
  93.9 0.4 copy-done.16
  94.3 6.3 %collective-permute-done.1 = bf16[4,128,512]{2,1,0:T(8,128)(2,1)} collective-permute-done((bf16[4,128,512]{2,1,0:T(8,128)(2,1)}, bf16[4,128,512]{2,1,0:T(8,128)(2,1)}, u32[]{:S(2)}, u32[]{:S(2)}) %collective-permute-start.1) | collective-permute-done | bytes 524320 | tf_op jit(solution)/shard_map/ppermute | solution.py:265
  100.6 1.3 multiply_add_fusion.2
  101.9 0.1 fusion.29
  102.0 3.4 %collective-permute-start.2 = (bf16[4,512,128]{2,1,0:T(8,128)(2,1)S(1)}, bf16[4,512,128]{2,1,0:T(8,128)(2,1)S(1)}, u32[]{:S(2)}, u32[]{:S(2)}) collective-permute-start(bf16[4,512,128]{2,1,0:T(8,128)(2,1)S(1)} %get-tuple-element.15), channel_id=1, source_target_pairs={{0,1},{1,2},{2,3},{3,4},{4,5},{5,6},{6,7},{8,9},{9,10},{10,11},{11... | collective-permute-start | bytes 1572872 | tf_op jit(solution)/shard_map/ppermute | solution.py:265
  105.5 13.3 %collective-permute-done.2 = bf16[4,512,128]{2,1,0:T(8,128)(2,1)S(1)} collective-permute-done((bf16[4,512,128]{2,1,0:T(8,128)(2,1)S(1)}, bf16[4,512,128]{2,1,0:T(8,128)(2,1)S(1)}, u32[]{:S(2)}, u32[]{:S(2)}) %collective-permute-start.2) | collective-permute-done | bytes 524320 | tf_op jit(solution)/shard_map/ppermute | solution.py:265
  118.8 0.2 multiply_add_fusion.1
  118.9 1.9 %collective-permute-start.3 = (bf16[4,512,128]{2,1,0:T(8,128)(2,1)S(1)}, bf16[4,512,128]{2,1,0:T(8,128)(2,1)S(1)}, u32[]{:S(2)}, u32[]{:S(2)}) collective-permute-start(bf16[4,512,128]{2,1,0:T(8,128)(2,1)S(1)} %get-tuple-element.14), channel_id=1, source_target_pairs={{1,0},{2,1},{3,2},{4,3},{5,4},{6,5},{7,6},{9,8},{10,9},{11,10},{12... | collective-permute-start | bytes 1572872 | tf_op jit(solution)/shard_map/ppermute | solution.py:265
  120.9 10.0 %collective-permute-done.3 = bf16[4,512,128]{2,1,0:T(8,128)(2,1)S(1)} collective-permute-done((bf16[4,512,128]{2,1,0:T(8,128)(2,1)S(1)}, bf16[4,512,128]{2,1,0:T(8,128)(2,1)S(1)}, u32[]{:S(2)}, u32[]{:S(2)}) %collective-permute-start.3) | collective-permute-done | bytes 524320 | tf_op jit(solution)/shard_map/ppermute | solution.py:265
  130.9 0.1 multiply_add_fusion
  131.1 2.3 %fusion.1 = f32[4,512,512]{2,1,0:T(8,128)} fusion(f32[4,128,512]{2,1,0:T(8,128)S(1)} %multiply_add_fusion.2, f32[4,256,512]{2,1,0:T(8,128)S(1)} %fusion.15, f32[4,128,512]{2,1,0:T(8,128)S(1)} %get-tuple-element.17, f32[4,512,128]{2,1,0:T(8,128)S(1)} %multiply_add_fusion, f32[4,512,128]{2,1,0:T(8,128)S(1)} %get-tuple-element.13), kind=kLoop, calls=%fused_computation.4 | loop fusion | flops 10485760 | bytes 10485760 | tf_op jit(solution)/shard_map/concatenate | solution.py:282
  (22 shorter events, 0.1 us)
Async XLA Ops:
  0.0 1.1 copy-start.2
  1.1 0.8 copy-start.3
  1.9 0.8 copy-start.4
  2.7 0.7 copy-start.7
  10.2 1.1 copy-start
  11.4 0.6 copy-start.6
  55.8 1.4 %copy-start.1 = (bf16[2,8,384,128]{3,2,1,0:T(8,128)(2,1)S(1)}, bf16[2,8,384,128]{3,2,1,0:T(8,128)(2,1)}, u32[]{:S(2)}) copy-start(bf16[2,8,384,128]{3,2,1,0:T(8,128)(2,1)} %get-tuple-element.11.tiles_ref) | copy-start | bytes 4718596
  57.3 0.8 copy-start.5
  58.0 9.2 %copy-start.10 = (bf16[1024,512]{1,0:T(8,128)(2,1)S(1)}, bf16[1024,512]{1,0:T(8,128)(2,1)}, u32[]{:S(2)}) copy-start(bf16[1024,512]{1,0:T(8,128)(2,1)} %constant.55) | copy-start | bytes 3145732
  67.2 1.2 copy-start.11
  68.4 1.2 copy-start.8
  68.4 1.5 %copy-start.9 = (f32[512,512]{0,1:T(8,128)S(1)}, f32[512,512]{0,1:T(8,128)}, u32[]{:S(2)}) copy-start(f32[512,512]{0,1:T(8,128)} %constant.42.clone) | copy-start | bytes 3145732
  68.4 1.5 %copy-start.14 = (f32[512]{0:T(512)S(1)}, f32[512]{0:T(512)}, u32[]{:S(2)}) copy-start(f32[512]{0:T(512)} %constant.57) | copy-start | bytes 6148
  68.4 1.5 %copy-start.15 = (f32[512]{0:T(512)S(1)}, f32[512]{0:T(512)}, u32[]{:S(2)}) copy-start(f32[512]{0:T(512)} %constant.54) | copy-start | bytes 6148
  70.0 1.2 copy-start.19
  71.2 1.3 copy-start.12
  73.8 1.6 %copy-start.18 = (bf16[1024,1024]{1,0:T(8,128)(2,1)S(1)}, bf16[1024,1024]{1,0:T(8,128)(2,1)}, u32[]{:S(2)}) copy-start(bf16[1024,1024]{1,0:T(8,128)(2,1)} %constant.47.clone) | copy-start | bytes 6291460
  77.9 2.0 %copy-start.17 = (f32[128]{0:T(128)S(1)}, f32[128]{0:T(128)}, u32[]{:S(2)}) copy-start(f32[128]{0:T(128)} %constant.48.clone) | copy-start | bytes 1540
  78.0 10.9 %collective-permute-start = (bf16[4,128,512]{2,1,0:T(8,128)(2,1)S(1)}, bf16[4,128,512]{2,1,0:T(8,128)(2,1)S(1)}, u32[]{:S(2)}, u32[]{:S(2)}) collective-permute-start(bf16[4,128,512]{2,1,0:T(8,128)(2,1)S(1)} %pad_maximum_fusion.5), channel_id=1, source_target_pairs={{0,8},{8,16},{16,24},{1,9},{9,17},{17,25},{2,10},{10,18},{18,26},{... | collective-permute-start | bytes 1572872 | tf_op jit(solution)/shard_map/ppermute | solution.py:265
  88.9 0.8 copy-start.13
  91.7 8.9 %collective-permute-start.1 = (bf16[4,128,512]{2,1,0:T(8,128)(2,1)}, bf16[4,128,512]{2,1,0:T(8,128)(2,1)}, u32[]{:S(2)}, u32[]{:S(2)}) collective-permute-start(bf16[4,128,512]{2,1,0:T(8,128)(2,1)} %get-tuple-element.18), channel_id=1, source_target_pairs={{8,0},{16,8},{24,16},{9,1},{17,9},{25,17},{10,2},{18,10},{26,18},{... | collective-permute-start | bytes 1572872 | tf_op jit(solution)/shard_map/ppermute | solution.py:265
  93.6 0.7 copy-start.16
  102.0 16.7 %collective-permute-start.2 = (bf16[4,512,128]{2,1,0:T(8,128)(2,1)S(1)}, bf16[4,512,128]{2,1,0:T(8,128)(2,1)S(1)}, u32[]{:S(2)}, u32[]{:S(2)}) collective-permute-start(bf16[4,512,128]{2,1,0:T(8,128)(2,1)S(1)} %get-tuple-element.15), channel_id=1, source_target_pairs={{0,1},{1,2},{2,3},{3,4},{4,5},{5,6},{6,7},{8,9},{9,10},{10,11},{11... | collective-permute-start | bytes 1572872 | tf_op jit(solution)/shard_map/ppermute | solution.py:265
  118.9 12.0 %collective-permute-start.3 = (bf16[4,512,128]{2,1,0:T(8,128)(2,1)S(1)}, bf16[4,512,128]{2,1,0:T(8,128)(2,1)S(1)}, u32[]{:S(2)}, u32[]{:S(2)}) collective-permute-start(bf16[4,512,128]{2,1,0:T(8,128)(2,1)S(1)} %get-tuple-element.14), channel_id=1, source_target_pairs={{1,0},{2,1},{3,2},{4,3},{5,4},{6,5},{7,6},{9,8},{10,9},{11,10},{12... | collective-permute-start | bytes 1572872 | tf_op jit(solution)/shard_map/ppermute | solution.py:265

commit v2 on v1

v2 whole, which is shorter than its diff:
```python
import functools
import math

import jax
import jax.numpy as jnp
import numpy as np
from jax import lax
from jax.experimental import pallas as pl
from jax.experimental.pallas import tpu as pltpu
from jax.sharding import PartitionSpec as P

PATCH = 512
MESH = pl.DeviceIdType.MESH
STEP = 16
PLACE = 512
TABLES = 7


def dft_tables(length):
    positions = np.arange(length)
    angles = (positions[:, None] * positions[None, :] % length).astype(np.float32) * np.float32(
        2.0 * math.pi / length
    )
    return np.cos(angles).astype(np.float32), np.sin(angles).astype(np.float32)


def wavenumbers(length):
    positions = np.arange(length)
    return (positions - length * (positions >= (length + 1) // 2)).astype(np.float32) * np.float32(2.0 / length)


def transform_tables(n):
    h = n // 2
    cos, sin = dft_tables(n)
    forward = np.concatenate([cos[:, :h], sin[:, :h]], 1)
    forward[:, h] = cos[:, h]
    down = np.concatenate([cos, sin], 0)
    back_rows = np.block([[cos, -sin], [sin, cos]])
    back_cols = np.concatenate([2.0 * cos[:h], -2.0 * sin[:h]], 0)
    back_cols[0] = 1.0
    back_cols[h] = cos[h]
    signed = wavenumbers(n).astype(np.float64)
    order = np.arange(1, h)
    lag = np.arange(n)
    wave = -(2.0 / n) * (signed[1:h] * np.sin(2.0 * np.pi * (lag[:, None] * order % n) / n)).sum(1)
    slope = wave[(lag[None, :] - lag[:, None]) % n]
    across, along = signed[None, :], signed[:, None]
    power = across**2 + along**2
    lens = 1j * (across + 1j * along) ** 3 / np.where(power > 0, power, 1.0) / (n * n)
    mirror = np.conj(lens[-lag % n][:, -lag % n])
    even, odd = (lens + mirror) / 2, (lens - mirror) / 2j
    weights = np.stack([even.real, even.imag, odd.real, odd.imag])
    edge = np.zeros((4, n, 128))
    edge[:, :, 0] = weights[:, :, h]
    bf16 = [jnp.asarray(t, jnp.bfloat16) for t in (forward, down, back_rows, back_cols, slope)]
    return *bf16, jnp.asarray(weights[:, :, :h], jnp.float32), jnp.asarray(edge, jnp.float32)


def blocked_dot(rows, left, right, write, block=256):
    def one(t, carry):
        start = pl.multiple_of(t * block, block)
        write(start, jnp.dot(left[pl.ds(start, block), :], right[...], preferred_element_type=jnp.float32))
        return carry

    lax.fori_loop(0, rows // block, one, 0)


def flexion_kernel(n_px, n_py, kappa, lists, slots, counts, *rest):
    sources, (out,), rest = rest[:TABLES], rest[TABLES : TABLES + 1], rest[TABLES + 1 :]
    slope, forward, down, weights, edge, back_rows, back_cols = tables = rest[:TABLES]
    (
        held, wide, stage, tiles, aux, got_tiles, got_aux, rows, marks, totals,
        patch, image, halves, spectrum, spectra, columns, fields, from_rows, from_cols, corners,
        load, send_t, recv_t, send_a, recv_a, send_v, recv_v, send_h, recv_h,
    ) = rest[TABLES:]
    i = lax.axis_index("px")
    j = lax.axis_index("py")
    cap = rows.shape[2]
    tile = wide.shape[1]
    n, h = PATCH, PATCH // 2
    slot_count = n * n // tile
    f32, bf16 = jnp.float32, jnp.bfloat16
    has_up, has_down = i > 0, i < n_px - 1
    upper = jnp.maximum(i - 1, 0)

    loads = [
        pltpu.make_async_copy(kappa, held, load.at[0]),
        pltpu.make_async_copy(counts, totals, load.at[1]),
    ]
    for b, band in enumerate((i, upper)):
        part = pl.ds(pl.multiple_of(band * n_py, n_py), n_py)
        loads.append(pltpu.make_async_copy(lists.at[0, part], rows.at[b], load.at[2 + b]))
        loads.append(pltpu.make_async_copy(slots.at[0, part], marks.at[b], load.at[4 + b]))
    table_loads = [
        pltpu.make_async_copy(a, b, load.at[6 + k]) for k, (a, b) in enumerate(zip(sources, tables))
    ]
    for copy in loads:
        copy.start()

    barrier = pltpu.get_barrier_semaphore()
    for o in range(1, n_py):
        pl.semaphore_signal(barrier, inc=1, device_id=(i, lax.rem(j + o, n_py)), device_id_type=MESH)

    @pl.when(has_down)
    def _():
        for o in range(n_py):
            pl.semaphore_signal(
                barrier, inc=1, device_id=(i + 1, lax.rem(j + o, n_py)), device_id_type=MESH
            )

    @pl.when(has_up)
    def _():
        pl.semaphore_signal(barrier, inc=1, device_id=(i - 1, j), device_id_type=MESH)

    for copy in loads:
        copy.wait()
    for copy in table_loads:
        copy.start()
    wide[...] = held[...].astype(f32)
    patch[...] = jnp.zeros_like(patch)
    pl.semaphore_wait(
        barrier, n_py - 1 + jnp.where(has_up, n_py, 0) + jnp.where(has_down, 1, 0)
    )

    def copies(b, o):
        target = (i - b, lax.rem(j + o, n_py))
        return [
            pltpu.make_async_remote_copy(
                src_ref=source.at[b, o],
                dst_ref=landing.at[b, o],
                send_sem=send.at[b, o],
                recv_sem=recv.at[b, o],
                device_id=target,
                device_id_type=MESH,
            )
            for source, landing, send, recv in (
                (tiles, got_tiles, send_t, recv_t),
                (aux, got_aux, send_a, recv_a),
            )
        ]

    lanes = lax.broadcasted_iota(jnp.int32, (1, cap), 1)

    def collect(b, o):
        column = lax.rem(j + o, n_py)

        def some(c, carry):
            base = pl.multiple_of(c * STEP, STEP)
            picks = [rows[b, column, base + k] for k in range(STEP)]
            values = [wide[pl.ds(pick, 1), :] for pick in picks]
            for k in range(STEP):
                stage[pl.ds(base + k, 1), :] = values[k]
            return carry

        lax.fori_loop(0, cap // STEP, some, 0)
        tiles[b, o] = stage[...].astype(bf16)
        count = totals[0, (i if b == 0 else upper) * n_py + column]
        aux[b, o] = jnp.where(lanes < count, marks[b, pl.ds(column, 1), :], slot_count)

    def place_of(t):
        step = (t + 1) // 2
        return lax.rem(n_py // 2 + step * (2 * lax.rem(t, 2) - 1) + n_py, n_py)

    def deliver(t, carry):
        o = place_of(t)
        collect(0, o)

        @pl.when(o > 0)
        def _():
            for copy in copies(0, o):
                copy.start()

        @pl.when(has_up)
        def _():
            collect(1, o)
            for copy in copies(1, o):
                copy.start()

        return carry

    lax.fori_loop(0, n_py, deliver, 0)

    def place(values, targets):
        def part(r, carry):
            base = pl.multiple_of(r * PLACE, PLACE)
            ids = lax.broadcasted_iota(jnp.int32, (PLACE, cap), 0) + base
            chosen = jnp.where(ids == targets, 1.0, 0.0).astype(bf16)
            patch[pl.ds(base, PLACE), :] += jnp.dot(chosen, values, preferred_element_type=f32)
            return carry

        lax.fori_loop(0, slot_count // PLACE, part, 0)

    def receive(t, carry):
        o = place_of(t)

        @pl.when(o == 0)
        def _():
            place(tiles[0, 0], aux[0, 0])

        @pl.when(o > 0)
        def _():
            for copy in copies(0, o):
                copy.wait_recv()
            place(got_tiles[0, o], got_aux[0, o])

        @pl.when(has_down)
        def _():
            for copy in copies(1, o):
                copy.wait_recv()
            place(got_tiles[1, o], got_aux[1, o])

        return carry

    lax.fori_loop(0, n_py, receive, 0)
    per_row = n // tile
    for c in range(per_row):
        image[:, c * tile : (c + 1) * tile] = patch[pl.ds(c, n, stride=per_row), :].astype(bf16)
    for copy in table_loads:
        copy.wait()

    width = tile
    has = [has_up, has_down, j > 0, j < n_py - 1]
    beside = [(i - 1, j), (i + 1, j), (i, j - 1), (i, j + 1)]
    ends = [pl.ds(0, width), pl.ds(n - width, width)]
    inner = pl.ds(width, n - 2 * width)
    pairs = [pl.ds(0, 2), pl.ds(2, 2)]

    def row_copy(side, pair):
        return pltpu.make_async_remote_copy(
            src_ref=fields.at[pairs[pair], ends[side], :],
            dst_ref=from_rows.at[1 - side, pairs[pair]],
            send_sem=send_v.at[side, pair],
            recv_sem=recv_v.at[1 - side, pair],
            device_id=beside[side],
            device_id_type=MESH,
        )

    def col_copy(side, piece):
        if piece < 2:
            part, span = pl.ds(0, 4), ends[piece]
            source = corners.at[side, :, span, :]
        else:
            part, span = pairs[piece - 2], inner
            source = fields.at[part, inner, ends[side]]
        return pltpu.make_async_remote_copy(
            src_ref=source,
            dst_ref=from_cols.at[1 - side, part, span, :],
            send_sem=send_h.at[side, piece],
            recv_sem=recv_h.at[1 - side, piece],
            device_id=beside[2 + side],
            device_id_type=MESH,
        )

    def send_strips(pair):
        for side in range(2):

            @pl.when(has[side])
            def _():
                row_copy(side, pair).start()

            @pl.when(has[2 + side])
            def _():
                col_copy(side, 2 + pair).start()

    pixels = image[...].astype(f32)
    row_sign = 1.0 - 2.0 * (lax.broadcasted_iota(jnp.int32, (n, 1), 0) % 2).astype(f32)
    col_sign = 1.0 - 2.0 * (lax.broadcasted_iota(jnp.int32, (1, n), 1) % 2).astype(f32)
    row_edge = jnp.sum(pixels * row_sign, axis=0, keepdims=True) * (1.0 / n)

    def write_real(start, value):
        sign = 1.0 - 2.0 * (lax.broadcasted_iota(jnp.int32, (value.shape[0], 1), 0) % 2).astype(f32)
        fields[0, pl.ds(start, value.shape[0]), :] = (value + sign * row_edge).astype(bf16)

    def write_imag(start, value):
        own = image[pl.ds(start, value.shape[0]), :].astype(f32)
        col_edge = jnp.sum(own * col_sign, axis=1, keepdims=True) * (1.0 / n)
        fields[1, pl.ds(start, value.shape[0]), :] = (-value - col_edge * col_sign).astype(bf16)

    blocked_dot(n, image, slope, write_real)
    blocked_dot(n, slope, image, write_imag)
    send_strips(0)

    def write_halves(start, value):
        halves[pl.ds(start, value.shape[0]), :] = value.astype(bf16)

    def write_spectrum(start, value):
        spectrum[pl.ds(start, value.shape[0]), :] = value

    blocked_dot(n, image, forward, write_halves)
    blocked_dot(2 * n, down, halves, write_spectrum)

    first = lax.broadcasted_iota(jnp.int32, (1, h), 1) == 0
    block = 64

    def multiply(t, carry):
        start = pl.multiple_of(t * block, block)
        low = pl.ds(start, block)
        high = pl.ds(pl.multiple_of(start + n, block), block)
        z_r = spectrum[low, :h] - jnp.where(first, 0.0, spectrum[high, h:])
        z_i = -(spectrum[high, :h] + jnp.where(first, 0.0, spectrum[low, h:]))
        e_r = spectrum[low, h : h + 128]
        e_i = -spectrum[high, h : h + 128]
        for s in range(2):
            k_r, k_i = weights[2 * s, low, :], weights[2 * s + 1, low, :]
            q_r, q_i = edge[2 * s, low, :], edge[2 * s + 1, low, :]
            g_r = k_r * z_r - k_i * z_i
            g_i = k_r * z_i + k_i * z_r
            top_r = q_r * e_r - q_i * e_i
            top_i = q_r * e_i + q_i * e_r
            spectra[low, s * h : s * h + 128] = (g_r[:, :128] - top_i).astype(bf16)
            spectra[low, s * h + 128 : (s + 1) * h] = g_r[:, 128:].astype(bf16)
            spectra[high, s * h : s * h + 128] = (g_i[:, :128] + top_r).astype(bf16)
            spectra[high, s * h + 128 : (s + 1) * h] = g_i[:, 128:].astype(bf16)
        return carry

    lax.fori_loop(0, n // block, multiply, 0)

    for part in range(2):

        def write_columns(start, value, part=part):
            rows = pl.ds(start, value.shape[0])
            for s in range(2):
                columns[s, rows, part * h : (part + 1) * h] = value[:, s * h : (s + 1) * h].astype(bf16)

        blocked_dot(n, back_rows.at[part], spectra, write_columns)
    for s in range(2):

        def write_three(start, value, s=s):
            fields[2 + s, pl.ds(start, value.shape[0]), :] = value.astype(bf16)

        blocked_dot(n, columns.at[s], back_cols, write_three)
    send_strips(1)

    out[:, inner, :] = fields[:, inner, :].astype(f32)

    def ramps(shape, dim):
        steps = lax.broadcasted_iota(jnp.int32, shape, dim).astype(f32)
        return (steps + 0.5) * (1.0 / width), (width - 0.5 - steps) * (1.0 / width)

    for side, ramp in enumerate(ramps((1, width, 1), 1)):
        span = ends[side]

        @pl.when(has[side])
        def _():
            for pair in range(2):
                row_copy(1 - side, pair).wait_recv()
            out[:, span, :] = ramp * fields[:, span, :].astype(f32) + (1.0 - ramp) * from_rows[
                side
            ].astype(f32)

        @pl.when(jnp.logical_not(has[side]))
        def _():
            out[:, span, :] = fields[:, span, :].astype(f32)

        for other in range(2):
            corners[other, :, span, :] = out[:, span, ends[other]].astype(bf16)

            @pl.when(has[2 + other])
            def _():
                col_copy(other, side).start()

    for piece in (2, 3, 0, 1):
        part, span = (pl.ds(0, 4), ends[piece]) if piece < 2 else (pairs[piece - 2], inner)
        for side, ramp in enumerate(ramps((1, 1, width), 2)):

            @pl.when(has[2 + side])
            def _():
                col_copy(1 - side, piece).wait_recv()
                out[part, span, ends[side]] = ramp * out[part, span, ends[side]] + (
                    1.0 - ramp
                ) * from_cols[side, part, span, :].astype(f32)

    for side in range(2):

        @pl.when(has[side])
        def _():
            for pair in range(2):
                row_copy(side, pair).wait_send()

        @pl.when(has[2 + side])
        def _():
            for piece in range(4):
                col_copy(side, piece).wait_send()

    def finish(t, carry):
        o = place_of(t)

        @pl.when(o > 0)
        def _():
            for copy in copies(0, o):
                copy.wait_send()

        @pl.when(has_up)
        def _():
            for copy in copies(1, o):
                copy.wait_send()

        return carry

    lax.fori_loop(0, n_py, finish, 0)


def on_device(kappa, send_list, dest_slot, send_count):
    n_px = lax.axis_size("px")
    n_py = lax.axis_size("py")
    cap = send_list.shape[2]
    tile = kappa.shape[1]
    n = PATCH
    forward, down, back_rows, back_cols, slope, weights, edge = transform_tables(n)
    tables = [slope, forward, down, weights, edge, back_rows.reshape(2, n, 2 * n), back_cols]
    anywhere = pl.BlockSpec(memory_space=pl.ANY)
    vmem, bf16, f32 = pltpu.VMEM, jnp.bfloat16, jnp.float32
    dma = pltpu.SemaphoreType.DMA
    tiles, aux = (2, n_py, cap, tile), (2, n_py, 1, cap)
    return pl.pallas_call(
        functools.partial(flexion_kernel, n_px, n_py),
        out_shape=jax.ShapeDtypeStruct((4, n, n), f32),
        in_specs=[anywhere] * (4 + TABLES),
        out_specs=pl.BlockSpec(memory_space=vmem),
        scratch_shapes=[vmem(table.shape, table.dtype) for table in tables]
        + [
            vmem(kappa.shape, bf16),
            vmem(kappa.shape, f32),
            vmem((cap, tile), f32),
            vmem(tiles, bf16),
            vmem(aux, jnp.int32),
            vmem(tiles, bf16),
            vmem(aux, jnp.int32),
            pltpu.SMEM((2, n_py, cap), jnp.int32),
            vmem((2, n_py, cap), jnp.int32),
            pltpu.SMEM(send_count.shape, jnp.int32),
            vmem((n * n // tile, tile), f32),
            vmem((n, n), bf16),
            vmem((n, n), bf16),
            vmem((2 * n, n), f32),
            vmem((2 * n, n), bf16),
            vmem((2, n, n), bf16),
            vmem((4, n, n), bf16),
            vmem((2, 4, tile, n), bf16),
            vmem((2, 4, n, tile), bf16),
            vmem((2, 4, n, tile), bf16),
            dma((6 + TABLES,)),
        ]
        + [dma((2, n_py))] * 4
        + [dma((2, 2))] * 2
        + [dma((2, 4))] * 2,
        compiler_params=pltpu.CompilerParams(
            collective_id=0, has_side_effects=True, vmem_limit_bytes=58 * 2**20
        ),
        name="flexion",
    )(kappa, send_list, dest_slot, send_count, *tables)


def solution(mesh):
    placed = (
        P(("px", "py"), None),
        P(("px", "py"), None, None),
        P(("px", "py"), None, None),
        P(("px", "py"), None),
    )
    return jax.shard_map(
        on_device, mesh=mesh, in_specs=placed, out_specs=P(None, "px", "py"), check_vma=False
    )
```

time: 135 us -> 79.5 us (0.59)
  the two profiles are of different devices: /device:TPU:14 before, /device:TPU:9 now
where the time goes in v2:
time: 79.5 us; the launch traced here: 78.1 us
  Pallas kernels  73.5 us (92%)
  local copies, waits for them, and re-layouts  4.64 us (6%)
    pallas_call x1, Pallas kernels, on_device(): pl.pallas_call(functools.partial(flexion_kernel, n_px, n_py), out_shape=j...  73.5 us
    unnamed x1, local copies, waits for them, and re-layouts  4.64 us

profile of v2, /device:TPU:9, one launch (start us, length us, event | category | flops | bytes accessed | tf_op | source)
XLA Modules:
  0.0 78.1 jit_solution(11745354873773746827)
XLA Ops:
  0.0 73.5 %flexion.1 = f32[4,512,512]{2,1,0:T(8,128)} custom-call(bf16[2400,128]{1,0:T(8,128)(2,1)} %kappa.1, s32[1,32,384]{2,1,0:T(8,128)} %lists.1, s32[1,32,384]{2,1,0:T(8,128)} %slots.1, s32[1,32]{1,0:T(1,128)} %counts.1, bf16[512,512]{1,0:T(8,128)(2,1)} %constant.18.clone.rest_0_, bf16[512,512]{1,0:T(8,128)(2,1)} %constant.14.clone.rest_1_, ...), custom_call_target="tpu_custom_call" | custom-call | tf_op jit(solution)/shard_map/flexion/pallas_call | solution.py:415
  73.5 4.6 %copy.13 = f32[4,512,512]{2,1,0:T(8,128)} copy(f32[4,512,512]{2,1,0:T(8,128)} %flexion.1) | data formatting | bytes 8388608

commit v3 on v2

--- a/solution.py
+++ b/solution.py
@@ -13,7 +13,7 @@
 MESH = pl.DeviceIdType.MESH
 STEP = 16
 PLACE = 512
-TABLES = 7
+RAISED = 128
 
 
 def dft_tables(length):
@@ -34,8 +34,6 @@
     cos, sin = dft_tables(n)
     forward = np.concatenate([cos[:, :h], sin[:, :h]], 1)
     forward[:, h] = cos[:, h]
-    down = np.concatenate([cos, sin], 0)
-    back_rows = np.block([[cos, -sin], [sin, cos]])
     back_cols = np.concatenate([2.0 * cos[:h], -2.0 * sin[:h]], 0)
     back_cols[0] = 1.0
     back_cols[h] = cos[h]
@@ -44,16 +42,7 @@
     lag = np.arange(n)
     wave = -(2.0 / n) * (signed[1:h] * np.sin(2.0 * np.pi * (lag[:, None] * order % n) / n)).sum(1)
     slope = wave[(lag[None, :] - lag[:, None]) % n]
-    across, along = signed[None, :], signed[:, None]
-    power = across**2 + along**2
-    lens = 1j * (across + 1j * along) ** 3 / np.where(power > 0, power, 1.0) / (n * n)
-    mirror = np.conj(lens[-lag % n][:, -lag % n])
-    even, odd = (lens + mirror) / 2, (lens - mirror) / 2j
-    weights = np.stack([even.real, even.imag, odd.real, odd.imag])
-    edge = np.zeros((4, n, 128))
-    edge[:, :, 0] = weights[:, :, h]
-    bf16 = [jnp.asarray(t, jnp.bfloat16) for t in (forward, down, back_rows, back_cols, slope)]
-    return *bf16, jnp.asarray(weights[:, :, :h], jnp.float32), jnp.asarray(edge, jnp.float32)
+    return jnp.asarray(np.concatenate([slope, forward, back_cols, cos, sin], 0), jnp.bfloat16)
 
 
 def blocked_dot(rows, left, right, write, block=256):
@@ -66,13 +55,14 @@
 
 
 def flexion_kernel(n_px, n_py, kappa, lists, slots, counts, *rest):
-    sources, (out,), rest = rest[:TABLES], rest[TABLES : TABLES + 1], rest[TABLES + 1 :]
-    slope, forward, down, weights, edge, back_rows, back_cols = tables = rest[:TABLES]
+    source, out, table, back_rows, weights = rest[:5]
+    slope, forward, back_cols = [table.at[pl.ds(k * PATCH, PATCH)] for k in range(3)]
+    down = table.at[pl.ds(3 * PATCH, 2 * PATCH)]
     (
-        held, wide, stage, tiles, aux, got_tiles, got_aux, rows, marks, totals,
+        held, wide, stage, tiles, aux, got_tiles, got_aux, rows, marks, totals, packed, bundle, bundle_to, far, far_to,
         patch, image, halves, spectrum, spectra, columns, fields, from_rows, from_cols, corners,
-        load, send_t, recv_t, send_a, recv_a, send_v, recv_v, send_h, recv_h,
-    ) = rest[TABLES:]
+        load, send_t, recv_t, send_a, recv_a, send_v, recv_v, send_h, recv_h, send_b, recv_b,
+    ) = rest[5:]
     i = lax.axis_index("px")
     j = lax.axis_index("py")
     cap = rows.shape[2]
@@ -82,6 +72,13 @@
     f32, bf16 = jnp.float32, jnp.bfloat16
     has_up, has_down = i > 0, i < n_px - 1
     upper = jnp.maximum(i - 1, 0)
+    half = n_py // 2
+    within = lax.rem(j, half)
+    base_near = j - within
+    partner = lax.rem(j + half, n_py)
+
+    def near(r):
+        return base_near + lax.rem(within + r, half)
 
     loads = [
         pltpu.make_async_copy(kappa, held, load.at[0]),
@@ -91,9 +88,7 @@
         part = pl.ds(pl.multiple_of(band * n_py, n_py), n_py)
         loads.append(pltpu.make_async_copy(lists.at[0, part], rows.at[b], load.at[2 + b]))
         loads.append(pltpu.make_async_copy(slots.at[0, part], marks.at[b], load.at[4 + b]))
-    table_loads = [
-        pltpu.make_async_copy(a, b, load.at[6 + k]) for k, (a, b) in enumerate(zip(sources, tables))
-    ]
+    table_load = pltpu.make_async_copy(source, table, load.at[6])
     for copy in loads:
         copy.start()
 
@@ -103,10 +98,8 @@
 
     @pl.when(has_down)
     def _():
-        for o in range(n_py):
-            pl.semaphore_signal(
-                barrier, inc=1, device_id=(i + 1, lax.rem(j + o, n_py)), device_id_type=MESH
-            )
+        for r in range(half):
+            pl.semaphore_signal(barrier, inc=1, device_id=(i + 1, near(r)), device_id_type=MESH)
 
     @pl.when(has_up)
     def _():
@@ -114,16 +107,15 @@
 
     for copy in loads:
         copy.wait()
-    for copy in table_loads:
-        copy.start()
+    table_load.start()
     wide[...] = held[...].astype(f32)
     patch[...] = jnp.zeros_like(patch)
     pl.semaphore_wait(
-        barrier, n_py - 1 + jnp.where(has_up, n_py, 0) + jnp.where(has_down, 1, 0)
+        barrier, n_py - 1 + jnp.where(has_up, half, 0) + jnp.where(has_down, 1, 0)
     )
 
     def copies(b, o):
-        target = (i - b, lax.rem(j + o, n_py))
+        target = (i, lax.rem(j + o, n_py)) if b == 0 else (i - 1, near(lax.rem(o, half)))
         return [
             pltpu.make_async_remote_copy(
                 src_ref=source.at[b, o],
@@ -142,7 +134,10 @@
     lanes = lax.broadcasted_iota(jnp.int32, (1, cap), 1)
 
     def collect(b, o):
-        column = lax.rem(j + o, n_py)
+        if b == 0:
+            column = lax.rem(j + o, n_py)
+        else:
+            column = lax.rem(near(lax.rem(o, half)) + half * (1 - o // half), n_py)
 
         def some(c, carry):
             base = pl.multiple_of(c * STEP, STEP)
@@ -172,24 +167,91 @@
 
         @pl.when(has_up)
         def _():
-            collect(1, o)
-            for copy in copies(1, o):
+            collect(1, t)
+            for copy in copies(1, t):
                 copy.start()
 
         return carry
 
     lax.fori_loop(0, n_py, deliver, 0)
+
+    table_load.wait()
+    back_rows[0, :, :n] = table[3 * n : 4 * n, :]
+    back_rows[0, :, n:] = -table[4 * n : 5 * n, :]
+    back_rows[1, :, :n] = table[4 * n : 5 * n, :]
+    back_rows[1, :, n:] = table[3 * n : 4 * n, :]
+    block = 64
+
+    def multipliers(t, carry):
+        start = pl.multiple_of(t * block, block)
+        row = lax.broadcasted_iota(jnp.int32, (block, h + 128), 0) + start
+        col = lax.broadcasted_iota(jnp.int32, (block, h + 128), 1)
+        along = (row - jnp.where(row >= h, n, 0)).astype(f32) * (2.0 / n)
+        across = jnp.where(col < h, col, -h).astype(f32) * (2.0 / n)
+        power = across * across + along * along
+        scale = (1.0 / (n * n)) / jnp.where(power > 0, power, 1.0)
+        scale = jnp.where(col <= h, scale, 0.0)
+        weights[0, pl.ds(start, block), :] = (along * along - 3.0 * across * across) * along * scale
+        weights[1, pl.ds(start, block), :] = (across * across - 3.0 * along * along) * across * scale
+        return carry
+
+    lax.fori_loop(0, n // block, multipliers, 0)
 
     def place(values, targets):
         def part(r, carry):
             base = pl.multiple_of(r * PLACE, PLACE)
-            ids = lax.broadcasted_iota(jnp.int32, (PLACE, cap), 0) + base
+            ids = lax.broadcasted_iota(jnp.int32, (PLACE, targets.shape[1]), 0) + base
             chosen = jnp.where(ids == targets, 1.0, 0.0).astype(bf16)
             patch[pl.ds(base, PLACE), :] += jnp.dot(chosen, values, preferred_element_type=f32)
             return carry
 
         lax.fori_loop(0, slot_count // PLACE, part, 0)
 
+    raised = packed.shape[0]
+
+    def bundle_copies():
+        return [
+            pltpu.make_async_remote_copy(
+                src_ref=here,
+                dst_ref=there,
+                send_sem=send_b.at[k],
+                recv_sem=recv_b.at[k],
+                device_id=(i, partner),
+                device_id_type=MESH,
+            )
+            for k, (here, there) in enumerate(((bundle, far), (bundle_to, far_to)))
+        ]
+
+    @pl.when(has_down)
+    def _():
+        packed[...] = jnp.zeros_like(packed)
+        high_lane = lax.broadcasted_iota(jnp.int32, (8, cap), 0)
+
+        def pack(r, carry):
+            taken, digits = carry
+            for copy in copies(1, r):
+                copy.wait_recv()
+            targets = got_aux[1, r]
+            live = targets < slot_count
+            position = jnp.where(live, taken + lanes, -1)
+            ids = lax.broadcasted_iota(jnp.int32, (raised, cap), 0)
+            chosen = jnp.where(ids == position, 1.0, 0.0).astype(bf16)
+            packed[...] += jnp.dot(chosen, got_tiles[1, r], preferred_element_type=f32)
+            parts = jnp.where(high_lane == 0, targets // 256, jnp.where(high_lane == 1, targets % 256, 1))
+            digits += lax.dot_general(
+                parts.astype(f32).astype(bf16), chosen, (((1,), (1,)), ((), ())), preferred_element_type=f32
+            )
+            return taken + jnp.sum(live.astype(jnp.int32), axis=1, keepdims=True), digits
+
+        _, digits = lax.fori_loop(
+            0, half, pack, (jnp.zeros((1, 1), jnp.int32), jnp.zeros((8, raised), f32))
+        )
+        digits = digits.astype(jnp.int32)
+        bundle[...] = packed[...].astype(bf16)
+        bundle_to[...] = jnp.where(digits[2:3] > 0, digits[0:1] * 256 + digits[1:2], slot_count)
+        for copy in bundle_copies():
+            copy.start()
+
     def receive(t, carry):
         o = place_of(t)
 
@@ -203,21 +265,25 @@
                 copy.wait_recv()
             place(got_tiles[0, o], got_aux[0, o])
 
-        @pl.when(has_down)
-        def _():
-            for copy in copies(1, o):
+        @pl.when(jnp.logical_and(has_down, t >= half))
+        def _():
+            for copy in copies(1, t):
                 copy.wait_recv()
-            place(got_tiles[1, o], got_aux[1, o])
+            place(got_tiles[1, t], got_aux[1, t])
 
         return carry
 
     lax.fori_loop(0, n_py, receive, 0)
+
+    @pl.when(has_down)
+    def _():
+        for copy in bundle_copies():
+            copy.wait_recv()
+        place(far[...], far_to[...])
+
     per_row = n // tile
     for c in range(per_row):
         image[:, c * tile : (c + 1) * tile] = patch[pl.ds(c, n, stride=per_row), :].astype(bf16)
-    for copy in table_loads:
-        copy.wait()
-
     width = tile
     has = [has_up, has_down, j > 0, j < n_py - 1]
     beside = [(i - 1, j), (i + 1, j), (i, j - 1), (i, j + 1)]
@@ -290,7 +356,6 @@
     blocked_dot(2 * n, down, halves, write_spectrum)
 
     first = lax.broadcasted_iota(jnp.int32, (1, h), 1) == 0
-    block = 64
 
     def multiply(t, carry):
         start = pl.multiple_of(t * block, block)
@@ -300,13 +365,16 @@
         z_i = -(spectrum[high, :h] + jnp.where(first, 0.0, spectrum[low, h:]))
         e_r = spectrum[low, h : h + 128]
         e_i = -spectrum[high, h : h + 128]
-        for s in range(2):
-            k_r, k_i = weights[2 * s, low, :], weights[2 * s + 1, low, :]
-            q_r, q_i = edge[2 * s, low, :], edge[2 * s + 1, low, :]
-            g_r = k_r * z_r - k_i * z_i
-            g_i = k_r * z_i + k_i * z_r
-            top_r = q_r * e_r - q_i * e_i
-            top_i = q_r * e_i + q_i * e_r
+        k_r, k_i = weights[0, low, :h], weights[1, low, :h]
+        q_r, q_i = weights[0, low, h:], weights[1, low, h:]
+        last = lax.broadcasted_iota(jnp.int32, (block, 1), 0) + start == h
+        r_last, r_rest = jnp.where(last, k_r, 0.0), jnp.where(last, 0.0, k_r)
+        q_last, q_rest = jnp.where(last, q_r, 0.0), jnp.where(last, 0.0, q_r)
+        parts = (
+            (r_last * z_r - k_i * z_i, r_last * z_i + k_i * z_r, q_last * e_r, q_last * e_i),
+            (r_rest * z_i, -r_rest * z_r, q_i * e_r + q_rest * e_i, q_i * e_i - q_rest * e_r),
+        )
+        for s, (g_r, g_i, top_r, top_i) in enumerate(parts):
             spectra[low, s * h : s * h + 128] = (g_r[:, :128] - top_i).astype(bf16)
             spectra[low, s * h + 128 : (s + 1) * h] = g_r[:, 128:].astype(bf16)
             spectra[high, s * h : s * h + 128] = (g_i[:, :128] + top_r).astype(bf16)
@@ -331,7 +399,7 @@
         blocked_dot(n, columns.at[s], back_cols, write_three)
     send_strips(1)
 
-    out[:, inner, :] = fields[:, inner, :].astype(f32)
+    out[:, inner, :] = fields[:, inner, :]
 
     def ramps(shape, dim):
         steps = lax.broadcasted_iota(jnp.int32, shape, dim).astype(f32)
@@ -344,16 +412,15 @@
         def _():
             for pair in range(2):
                 row_copy(1 - side, pair).wait_recv()
-            out[:, span, :] = ramp * fields[:, span, :].astype(f32) + (1.0 - ramp) * from_rows[
-                side
-            ].astype(f32)
+            own, other = fields[:, span, :].astype(f32), from_rows[side].astype(f32)
+            out[:, span, :] = (ramp * own + (1.0 - ramp) * other).astype(bf16)
 
         @pl.when(jnp.logical_not(has[side]))
         def _():
-            out[:, span, :] = fields[:, span, :].astype(f32)
+            out[:, span, :] = fields[:, span, :]
 
         for other in range(2):
-            corners[other, :, span, :] = out[:, span, ends[other]].astype(bf16)
+            corners[other, :, span, :] = out[:, span, ends[other]]
 
             @pl.when(has[2 + other])
             def _():
@@ -366,9 +433,9 @@
             @pl.when(has[2 + side])
             def _():
                 col_copy(1 - side, piece).wait_recv()
-                out[part, span, ends[side]] = ramp * out[part, span, ends[side]] + (
-                    1.0 - ramp
-                ) * from_cols[side, part, span, :].astype(f32)
+                own = out[part, span, ends[side]].astype(f32)
+                other = from_cols[side, part, span, :].astype(f32)
+                out[part, span, ends[side]] = (ramp * own + (1.0 - ramp) * other).astype(bf16)
 
     for side in range(2):
 
@@ -398,6 +465,11 @@
         return carry
 
     lax.fori_loop(0, n_py, finish, 0)
+
+    @pl.when(has_down)
+    def _():
+        for copy in bundle_copies():
+            copy.wait_send()
 
 
 def on_device(kappa, send_list, dest_slot, send_count):
@@ -406,19 +478,20 @@
     cap = send_list.shape[2]
     tile = kappa.shape[1]
     n = PATCH
-    forward, down, back_rows, back_cols, slope, weights, edge = transform_tables(n)
-    tables = [slope, forward, down, weights, edge, back_rows.reshape(2, n, 2 * n), back_cols]
+    raised = RAISED * n // tile
     anywhere = pl.BlockSpec(memory_space=pl.ANY)
     vmem, bf16, f32 = pltpu.VMEM, jnp.bfloat16, jnp.float32
     dma = pltpu.SemaphoreType.DMA
     tiles, aux = (2, n_py, cap, tile), (2, n_py, 1, cap)
-    return pl.pallas_call(
+    blended = pl.pallas_call(
         functools.partial(flexion_kernel, n_px, n_py),
-        out_shape=jax.ShapeDtypeStruct((4, n, n), f32),
-        in_specs=[anywhere] * (4 + TABLES),
+        out_shape=jax.ShapeDtypeStruct((4, n, n), bf16),
+        in_specs=[anywhere] * 5,
         out_specs=pl.BlockSpec(memory_space=vmem),
-        scratch_shapes=[vmem(table.shape, table.dtype) for table in tables]
-        + [
+        scratch_shapes=[
+            vmem((5 * n, n), bf16),
+            vmem((2, n, 2 * n), bf16),
+            vmem((2, n, n // 2 + 128), f32),
             vmem(kappa.shape, bf16),
             vmem(kappa.shape, f32),
             vmem((cap, tile), f32),
@@ -429,6 +502,11 @@
             pltpu.SMEM((2, n_py, cap), jnp.int32),
             vmem((2, n_py, cap), jnp.int32),
             pltpu.SMEM(send_count.shape, jnp.int32),
+            vmem((raised, tile), f32),
+            vmem((raised, tile), bf16),
+            vmem((1, raised), jnp.int32),
+            vmem((raised, tile), bf16),
+            vmem((1, raised), jnp.int32),
             vmem((n * n // tile, tile), f32),
             vmem((n, n), bf16),
             vmem((n, n), bf16),
@@ -439,16 +517,18 @@
             vmem((2, 4, tile, n), bf16),
             vmem((2, 4, n, tile), bf16),
             vmem((2, 4, n, tile), bf16),
-            dma((6 + TABLES,)),
+            dma((7,)),
         ]
         + [dma((2, n_py))] * 4
         + [dma((2, 2))] * 2
-        + [dma((2, 4))] * 2,
+        + [dma((2, 4))] * 2
+        + [dma((2,))] * 2,
         compiler_params=pltpu.CompilerParams(
             collective_id=0, has_side_effects=True, vmem_limit_bytes=58 * 2**20
         ),
         name="flexion",
-    )(kappa, send_list, dest_slot, send_count, *tables)
+    )(kappa, send_list, dest_slot, send_count, transform_tables(n))
+    return blended.astype(f32)
 
 
 def solution(mesh):

time: 79.5 us -> 71 us (0.89); the launches traced: 78.1 us -> 70.9 us
  Pallas kernels: 73.5 us -> 66.7 us
  local copies, waits for them, and re-layouts: 4.64 us -> 0 us
  other arithmetic: 0 us -> 4.19 us
    pallas_call x1, Pallas kernels: 73.5 us -> 66.7 us  [on_device(): pl.pallas_call(functools.partial(flexion_kernel, n_px, n_py), out_shape=j...]
    unnamed x1 -> x0, local copies, waits for them, and re-layouts: 4.64 us -> none
    convert_element_type x0 -> x1, other arithmetic: none -> 4.19 us  [on_device(): return blended.astype(f32)]
where the time goes in v3:
time: 71 us; the launch traced here: 70.9 us
  Pallas kernels  66.7 us (94%)
  other arithmetic  4.19 us (6%)
    pallas_call x1, Pallas kernels, on_device(): pl.pallas_call(functools.partial(flexion_kernel, n_px, n_py), out_shape=j...  66.7 us
    convert_element_type x1, other arithmetic, on_device(): return blended.astype(f32)  4.19 us

profile of v3, /device:TPU:9, one launch (start us, length us, event | category | flops | bytes accessed | tf_op | source)
XLA Modules:
  0.0 70.9 jit_solution(3079582430876854411)
XLA Ops:
  0.0 66.7 %flexion.1 = bf16[4,512,512]{2,1,0:T(8,128)(2,1)} custom-call(bf16[2400,128]{1,0:T(8,128)(2,1)} %kappa.1, s32[1,32,384]{2,1,0:T(8,128)} %lists.1, s32[1,32,384]{2,1,0:T(8,128)} %slots.1, s32[1,32]{1,0:T(1,128)} %counts.1, bf16[2560,512]{1,0:T(8,128)(2,1)} %constant.2.clone.rest_0_), custom_call_target="tpu_custom_call" | custom-call | tf_op jit(solution)/shard_map/flexion/pallas_call | solution.py:486
  66.7 4.2 %convert_element_type.3 = f32[4,512,512]{2,1,0:T(8,128)} convert(bf16[4,512,512]{2,1,0:T(8,128)(2,1)} %flexion.1) | non-fusion elementwise | flops 1048576 | bytes 6291456 | tf_op jit(solution)/shard_map/convert_element_type | solution.py:531

commit v4 on v3

--- a/solution.py
+++ b/solution.py
@@ -12,7 +12,6 @@
 PATCH = 512
 MESH = pl.DeviceIdType.MESH
 STEP = 16
-PLACE = 512
 RAISED = 128
 
 
@@ -197,15 +196,17 @@
 
     lax.fori_loop(0, n // block, multipliers, 0)
 
+    per_row = n // tile
+
     def place(values, targets):
-        def part(r, carry):
-            base = pl.multiple_of(r * PLACE, PLACE)
-            ids = lax.broadcasted_iota(jnp.int32, (PLACE, targets.shape[1]), 0) + base
-            chosen = jnp.where(ids == targets, 1.0, 0.0).astype(bf16)
-            patch[pl.ds(base, PLACE), :] += jnp.dot(chosen, values, preferred_element_type=f32)
-            return carry
-
-        lax.fori_loop(0, slot_count // PLACE, part, 0)
+        count = targets.shape[1]
+        ids = lax.broadcasted_iota(jnp.int32, (n, count), 0)
+        chosen = jnp.where(ids == targets // per_row, 1.0, 0.0).astype(bf16)
+        block_of = jnp.transpose(jnp.broadcast_to(targets % per_row, (8, count)))[:, :1]
+        spread = jnp.concatenate(
+            [jnp.where(block_of == c, values, jnp.zeros_like(values)) for c in range(per_row)], axis=1
+        )
+        patch[...] += jnp.dot(chosen, spread, preferred_element_type=f32)
 
     raised = packed.shape[0]
 
@@ -252,28 +253,39 @@
         for copy in bundle_copies():
             copy.start()
 
-    def receive(t, carry):
-        o = place_of(t)
-
-        @pl.when(o == 0)
-        def _():
-            place(tiles[0, 0], aux[0, 0])
-
-        @pl.when(o > 0)
-        def _():
-            for copy in copies(0, o):
+    def two(b, a, c):
+        place(
+            jnp.concatenate([got_tiles[b, a], got_tiles[b, c]], axis=0),
+            jnp.concatenate([got_aux[b, a], got_aux[b, c]], axis=1),
+        )
+
+    def receive(u, carry):
+        first, second = place_of(2 * u), place_of(2 * u + 1)
+        for copy in copies(0, first):
+            copy.wait_recv()
+
+        @pl.when(second > 0)
+        def _():
+            for copy in copies(0, second):
                 copy.wait_recv()
-            place(got_tiles[0, o], got_aux[0, o])
-
-        @pl.when(jnp.logical_and(has_down, t >= half))
-        def _():
-            for copy in copies(1, t):
-                copy.wait_recv()
-            place(got_tiles[1, t], got_aux[1, t])
+
+        @pl.when(second == 0)
+        def _():
+            got_tiles[0, 0] = tiles[0, 0]
+            got_aux[0, 0] = aux[0, 0]
+
+        two(0, first, second)
+
+        @pl.when(jnp.logical_and(has_down, 2 * u >= half))
+        def _():
+            for t in (2 * u, 2 * u + 1):
+                for copy in copies(1, t):
+                    copy.wait_recv()
+            two(1, 2 * u, 2 * u + 1)
 
         return carry
 
-    lax.fori_loop(0, n_py, receive, 0)
+    lax.fori_loop(0, half, receive, 0)
 
     @pl.when(has_down)
     def _():
@@ -281,9 +293,8 @@
             copy.wait_recv()
         place(far[...], far_to[...])
 
-    per_row = n // tile
-    for c in range(per_row):
-        image[:, c * tile : (c + 1) * tile] = patch[pl.ds(c, n, stride=per_row), :].astype(bf16)
+    image[...] = patch[...].astype(bf16)
+
     width = tile
     has = [has_up, has_down, j > 0, j < n_py - 1]
     beside = [(i - 1, j), (i + 1, j), (i, j - 1), (i, j + 1)]
@@ -470,6 +481,10 @@
     def _():
         for copy in bundle_copies():
             copy.wait_send()
+
+
+def widen_kernel(narrow, out):
+    out[...] = narrow[...].astype(jnp.float32)
 
 
 def on_device(kappa, send_list, dest_slot, send_count):
@@ -507,7 +522,7 @@
             vmem((1, raised), jnp.int32),
             vmem((raised, tile), bf16),
             vmem((1, raised), jnp.int32),
-            vmem((n * n // tile, tile), f32),
+            vmem((n, n), f32),
             vmem((n, n), bf16),
             vmem((n, n), bf16),
             vmem((2 * n, n), f32),
@@ -528,7 +543,15 @@
         ),
         name="flexion",
     )(kappa, send_list, dest_slot, send_count, transform_tables(n))
-    return blended.astype(f32)
+    block = pl.BlockSpec((1, n // 2, n), lambda k, r: (k, r, 0))
+    return pl.pallas_call(
+        widen_kernel,
+        out_shape=jax.ShapeDtypeStruct((4, n, n), f32),
+        grid=(4, 2),
+        in_specs=[block],
+        out_specs=block,
+        name="widen",
+    )(blended)
 
 
 def solution(mesh):

time: 71 us -> 66.4 us (0.935)
  other arithmetic: 4.19 us -> 0 us
    pallas_call x1, Pallas kernels: 66.7 us -> 60.1 us  [on_device(): pl.pallas_call(functools.partial(flexion_kernel, n_px, n_py), out_shape=j...]
    pallas_call x0 -> x1, Pallas kernels: none -> 5.99 us  [on_device(): pl.pallas_call(widen_kernel, out_shape=jax.ShapeDtypeStruct((4, n, n), f3...]
    convert_element_type x1 -> x0, other arithmetic: 4.19 us -> none  [on_device(): return blended.astype(f32)]
where the time goes in v4:
time: 66.4 us; the launch traced here: 66.1 us
  Pallas kernels  66.1 us (100%)
    pallas_call x1, Pallas kernels, on_device(): pl.pallas_call(functools.partial(flexion_kernel, n_px, n_py), out_shape=j...  60.1 us
    pallas_call x1, Pallas kernels, on_device(): pl.pallas_call(widen_kernel, out_shape=jax.ShapeDtypeStruct((4, n, n), f3...  5.99 us

profile of v4, /device:TPU:9, one launch (start us, length us, event | category | flops | bytes accessed | tf_op | source)
XLA Modules:
  0.0 66.1 jit_solution(15938557139032349665)
XLA Ops:
  0.0 60.1 %flexion.1.narrow = bf16[4,512,512]{2,1,0:T(8,128)(2,1)} custom-call(bf16[2400,128]{1,0:T(8,128)(2,1)} %kappa.1, s32[1,32,384]{2,1,0:T(8,128)} %lists.1, s32[1,32,384]{2,1,0:T(8,128)} %slots.1, s32[1,32]{1,0:T(1,128)} %counts.1, bf16[2560,512]{1,0:T(8,128)(2,1)} %constant.2.clone.rest_0_), custom_call_target="tpu_custom_call" | custom-call | tf_op jit(solution)/shard_map/flexion/pallas_call | solution.py:501
  60.1 6.0 %widen.1 = f32[4,512,512]{2,1,0:T(8,128)} custom-call(bf16[4,512,512]{2,1,0:T(8,128)(2,1)} %flexion.1.narrow), custom_call_target="tpu_custom_call" | custom-call | tf_op jit(solution)/shard_map/widen/pallas_call | solution.py:547

commit v5 on v4

--- a/solution.py
+++ b/solution.py
@@ -174,27 +174,6 @@
 
     lax.fori_loop(0, n_py, deliver, 0)
 
-    table_load.wait()
-    back_rows[0, :, :n] = table[3 * n : 4 * n, :]
-    back_rows[0, :, n:] = -table[4 * n : 5 * n, :]
-    back_rows[1, :, :n] = table[4 * n : 5 * n, :]
-    back_rows[1, :, n:] = table[3 * n : 4 * n, :]
-    block = 64
-
-    def multipliers(t, carry):
-        start = pl.multiple_of(t * block, block)
-        row = lax.broadcasted_iota(jnp.int32, (block, h + 128), 0) + start
-        col = lax.broadcasted_iota(jnp.int32, (block, h + 128), 1)
-        along = (row - jnp.where(row >= h, n, 0)).astype(f32) * (2.0 / n)
-        across = jnp.where(col < h, col, -h).astype(f32) * (2.0 / n)
-        power = across * across + along * along
-        scale = (1.0 / (n * n)) / jnp.where(power > 0, power, 1.0)
-        scale = jnp.where(col <= h, scale, 0.0)
-        weights[0, pl.ds(start, block), :] = (along * along - 3.0 * across * across) * along * scale
-        weights[1, pl.ds(start, block), :] = (across * across - 3.0 * along * along) * across * scale
-        return carry
-
-    lax.fori_loop(0, n // block, multipliers, 0)
 
     per_row = n // tile
 
@@ -252,6 +231,28 @@
         bundle_to[...] = jnp.where(digits[2:3] > 0, digits[0:1] * 256 + digits[1:2], slot_count)
         for copy in bundle_copies():
             copy.start()
+
+    table_load.wait()
+    back_rows[0, :, :n] = table[3 * n : 4 * n, :]
+    back_rows[0, :, n:] = -table[4 * n : 5 * n, :]
+    back_rows[1, :, :n] = table[4 * n : 5 * n, :]
+    back_rows[1, :, n:] = table[3 * n : 4 * n, :]
+    block = 64
+
+    def multipliers(t, carry):
+        start = pl.multiple_of(t * block, block)
+        row = lax.broadcasted_iota(jnp.int32, (block, h + 128), 0) + start
+        col = lax.broadcasted_iota(jnp.int32, (block, h + 128), 1)
+        along = (row - jnp.where(row >= h, n, 0)).astype(f32) * (2.0 / n)
+        across = jnp.where(col < h, col, -h).astype(f32) * (2.0 / n)
+        power = across * across + along * along
+        scale = (1.0 / (n * n)) / jnp.where(power > 0, power, 1.0)
+        scale = jnp.where(col <= h, scale, 0.0)
+        weights[0, pl.ds(start, block), :] = (along * along - 3.0 * across * across) * along * scale
+        weights[1, pl.ds(start, block), :] = (across * across - 3.0 * along * along) * across * scale
+        return carry
+
+    lax.fori_loop(0, n // block, multipliers, 0)
 
     def two(b, a, c):
         place(
@@ -483,8 +484,24 @@
             copy.wait_send()
 
 
-def widen_kernel(narrow, out):
-    out[...] = narrow[...].astype(jnp.float32)
+def widen_kernel(narrow, out, held, wide, arrive, leave):
+    pieces = [(k, pl.ds(r, PATCH // 2)) for k in range(held.shape[0]) for r in (0, PATCH // 2)]
+    loads = [
+        pltpu.make_async_copy(narrow.at[k, rows], held.at[k, rows], arrive.at[t])
+        for t, (k, rows) in enumerate(pieces)
+    ]
+    stores = [
+        pltpu.make_async_copy(wide.at[k, rows], out.at[k, rows], leave.at[t])
+        for t, (k, rows) in enumerate(pieces)
+    ]
+    for copy in loads:
+        copy.start()
+    for load, store, (k, rows) in zip(loads, stores, pieces):
+        load.wait()
+        wide[k, rows] = held[k, rows].astype(jnp.float32)
+        store.start()
+    for copy in stores:
+        copy.wait()
 
 
 def on_device(kappa, send_list, dest_slot, send_count):
@@ -543,13 +560,13 @@
         ),
         name="flexion",
     )(kappa, send_list, dest_slot, send_count, transform_tables(n))
-    block = pl.BlockSpec((1, n // 2, n), lambda k, r: (k, r, 0))
     return pl.pallas_call(
         widen_kernel,
         out_shape=jax.ShapeDtypeStruct((4, n, n), f32),
-        grid=(4, 2),
-        in_specs=[block],
-        out_specs=block,
+        in_specs=[anywhere],
+        out_specs=anywhere,
+        scratch_shapes=[vmem((4, n, n), bf16), vmem((4, n, n), f32), dma((8,)), dma((8,))],
+        compiler_params=pltpu.CompilerParams(vmem_limit_bytes=58 * 2**20),
         name="widen",
     )(blended)
 

time: 66.4 us -> 63.7 us (0.959)
  Pallas kernels: 66.1 us -> 63.6 us
    pallas_call x1, Pallas kernels: 5.99 us -> 3.12 us  [on_device(): pl.pallas_call(widen_kernel, out_shape=jax.ShapeDtypeStruct((4, n, n), f3...]
where the time goes in v5:
time: 63.7 us; the launch traced here: 63.6 us
  Pallas kernels  63.6 us (100%)
    pallas_call x1, Pallas kernels, on_device(): pl.pallas_call(functools.partial(flexion_kernel, n_px, n_py), out_shape=j...  60.4 us
    pallas_call x1, Pallas kernels, on_device(): pl.pallas_call(widen_kernel, out_shape=jax.ShapeDtypeStruct((4, n, n), f3...  3.12 us

profile of v5, /device:TPU:9, one launch (start us, length us, event | category | flops | bytes accessed | tf_op | source)
XLA Modules:
  0.0 63.6 jit_solution(2903036762072532738)
XLA Ops:
  0.0 60.4 %flexion.1.narrow = bf16[4,512,512]{2,1,0:T(8,128)(2,1)} custom-call(bf16[2400,128]{1,0:T(8,128)(2,1)} %kappa.1, s32[1,32,384]{2,1,0:T(8,128)} %lists.1, s32[1,32,384]{2,1,0:T(8,128)} %slots.1, s32[1,32]{1,0:T(1,128)} %counts.1, bf16[2560,512]{1,0:T(8,128)(2,1)} %constant.2.clone.rest_0_), custom_call_target="tpu_custom_call" | custom-call | tf_op jit(solution)/shard_map/flexion/pallas_call | solution.py:518
  60.4 3.1 %widen.1 = f32[4,512,512]{2,1,0:T(8,128)} custom-call(bf16[4,512,512]{2,1,0:T(8,128)(2,1)} %flexion.1.narrow), custom_call_target="tpu_custom_call" | custom-call | tf_op jit(solution)/shard_map/widen/pallas_call | solution.py:563
